TPU v7x, 32 devices: a whole 2x2x4 slice. The times are simulated.
32 devices in a mesh: dp: 8 (over y, x, core), tensor: 4 (over z).
Axes of the slice: x: 2, y: 2, z: 4, core: 2. Of those that a mesh axis runs over, the one named last changes fastest.
Arguments:
- tokens_in: bfloat16 [8192, 768], P('dp'), may hold values from -6 to 6
- segments: int32 [8, 1024], P('dp'), may hold values from 0 to 3, never falling along the last dimension, each value on 1 to 512 neighbouring positions
- ln1_gain: float32 [768], replicated, may hold values from 0.1 to 1.9
- ln1_shift: float32 [768], replicated, may hold values from -3 to 3
- w_query: bfloat16 [768, 768], P(None, 'tensor'), may hold values from -0.21875 to 0.21875
- bias_query: float32 [768], P('tensor'), may hold values from -3 to 3
- w_key: bfloat16 [768, 768], P(None, 'tensor'), may hold values from -0.21875 to 0.21875
- w_value: bfloat16 [768, 768], P(None, 'tensor'), may hold values from -0.21875 to 0.21875
- bias_value: float32 [768], P('tensor'), may hold values from -3 to 3
- w_out: bfloat16 [768, 768], P('tensor'), may hold values from -1.75 to 1.75
- bias_out: float32 [768], replicated, may hold values from -3 to 3
- ln2_gain: float32 [768], replicated, may hold values from 0.1 to 1.9
- ln2_shift: float32 [768], replicated, may hold values from -3 to 3
- w_up: bfloat16 [768, 3072], P(None, 'tensor'), may hold values from -0.21875 to 0.21875
- bias_up: float32 [3072], P('tensor'), may hold values from -3 to 3
- w_down: bfloat16 [3072, 768], P('tensor'), may hold values from -0.109375 to 0.109375
- bias_down: float32 [768], replicated, may hold values from -3 to 3
- cotangent: bfloat16 [8192, 768], P('dp'), may hold values from -6 to 6
Outputs:
- output: bfloat16 [8192, 768], P('dp')
- grad_input: float32 [8192, 768], P('dp')
- grad_ln1_gain: float32 [768], replicated
- grad_ln1_shift: float32 [768], replicated
- grad_w_query: float32 [768, 768], P(None, 'tensor')
- grad_bias_query: float32 [768], P('tensor')
- grad_w_key: float32 [768, 768], P(None, 'tensor')
- grad_w_value: float32 [768, 768], P(None, 'tensor')
- grad_bias_value: float32 [768], P('tensor')
- grad_w_out: float32 [768, 768], P('tensor')
- grad_bias_out: float32 [768], replicated
- grad_ln2_gain: float32 [768], replicated
- grad_ln2_shift: float32 [768], replicated
- grad_w_up: float32 [768, 3072], P(None, 'tensor')
- grad_bias_up: float32 [3072], P('tensor')
- grad_w_down: float32 [3072, 768], P('tensor')
- grad_bias_down: float32 [768], replicated
Inputs may be any that keep to these rules, and one draw needn't show every extreme that they name: `segments`: within each sequence the document numbers never fall, each document holds 1 to half of 1024 tokens, and one holds exactly half of 1024.
All inputs are finite; a program needn't handle non-finite values.
Results may differ from a plain program's by a relative error of at most 0.012.
The roundings to bfloat16 on the way count: a program that leaves them out, or rounds other values in their place, can miss the bound.
Values sent between devices are 32-bit elements; how exact they have to be, the bound alone decides.
A program may use at most 128 MiB of HBM per device.

v0:
```python
import jax
import jax.numpy as jnp
from jax import lax
from jax.sharding import PartitionSpec as P

HD = 64


EPS = 1e-05
NEGATIVE = -1e30


def layer_norm(values, scale_vec, shift_vec):
    centre = values - jnp.mean(values, axis=-1, keepdims=True)
    spread = jnp.mean(centre * centre, axis=-1, keepdims=True)
    return centre * lax.rsqrt(spread + EPS) * scale_vec + shift_vec


def smooth_unit(values):
    return jax.nn.gelu(values, approximate=True)


def matmul(left_side, right_side):
    return jnp.dot(left_side, right_side, preferred_element_type=jnp.float32)


def inner_rows(left_side, right_side):
    return lax.dot_general(
        left_side, right_side, (((0,), (0,)), ((), ())), preferred_element_type=jnp.float32
    )


def inner_cols(left_side, right_side):
    return lax.dot_general(
        left_side, right_side, (((1,), (1,)), ((), ())), preferred_element_type=jnp.float32
    )


def heads_first(values, local_heads):
    return values.reshape(values.shape[0], local_heads, HD).transpose(1, 0, 2)


def heads_last(values):
    return values.transpose(1, 0, 2).reshape(values.shape[1], values.shape[0] * values.shape[2])


def block_scores(query_block, key_heads, labels, start_row, block_rows):
    seq_length = labels.shape[0]
    row_label = labels[start_row : start_row + block_rows]
    rows_at = start_row + jnp.arange(block_rows)[:, None]
    cols_at = jnp.arange(seq_length)[None, :]
    allowed = (rows_at >= cols_at) & (row_label[:, None] == labels[None, :])
    scores = jnp.einsum(
        "hqd,hkd->hqk", query_block, key_heads, preferred_element_type=jnp.float32
    ) * HD ** (-0.5)
    return jnp.where(allowed[None], scores, NEGATIVE)


def per_device(
    tokens_in,
    segments,
    ln1_gain,
    ln1_shift,
    w_query,
    bias_query,
    w_key,
    w_value,
    bias_value,
    w_out,
    bias_out,
    ln2_gain,
    ln2_shift,
    w_up,
    bias_up,
    w_down,
    bias_down,
    cotangent,
):
    inputs = tokens_in.astype(jnp.float32)
    local_heads = w_query.shape[1] // HD
    seq_count, seq_len = segments.shape
    block_rows = min(512, seq_len)
    normed_one, norm_one_back = jax.vjp(layer_norm, inputs, ln1_gain, ln1_shift)
    normed_low = normed_one.astype(jnp.bfloat16)
    query = (matmul(normed_low, w_query) + bias_query).astype(jnp.bfloat16)
    keys = matmul(normed_low, w_key).astype(jnp.bfloat16)
    values = (matmul(normed_low, w_value) + bias_value).astype(jnp.bfloat16)
    logsum_blocks = []
    seq_at = 0
    query_heads = heads_first(query, local_heads)
    key_heads = heads_first(keys, local_heads)
    value_heads = heads_first(values, local_heads)
    mixed_blocks = []
    for start_row in range(0, seq_len, block_rows):
        scores = block_scores(
            query_heads[:, start_row : start_row + block_rows],
            key_heads,
            segments[seq_at],
            start_row,
            block_rows,
        )
        row_top = jnp.max(scores, axis=-1, keepdims=True)
        exponent = jnp.exp(scores - row_top)
        row_total = jnp.sum(exponent, axis=-1, keepdims=True)
        chances = (exponent / row_total).astype(jnp.bfloat16)
        mixed_blocks.append(
            jnp.einsum("hqk,hkd->hqd", chances, value_heads, preferred_element_type=jnp.float32)
        )
        logsum_blocks.append(row_top + jnp.log(row_total))
    attended_seqs = heads_last(jnp.concatenate(mixed_blocks, axis=1))
    attended_low = attended_seqs.astype(jnp.bfloat16)
    attention_total = lax.psum(matmul(attended_low, w_out), "tensor")
    hidden_one = inputs + attention_total + bias_out
    normed_two, norm_two_back = jax.vjp(layer_norm, hidden_one, ln2_gain, ln2_shift)
    normed_two_low = normed_two.astype(jnp.bfloat16)
    pre_act = matmul(normed_two_low, w_up) + bias_up
    activated, act_back = jax.vjp(smooth_unit, pre_act)
    activated_low = activated.astype(jnp.bfloat16)
    feed_total = lax.psum(matmul(activated_low, w_down), "tensor")
    output = (hidden_one + feed_total + bias_down).astype(jnp.bfloat16)
    grad_out = cotangent.astype(jnp.float32)
    grad_w_down = inner_rows(activated_low, cotangent)
    grad_bias_down = jnp.sum(grad_out, axis=0)
    (grad_pre,) = act_back(inner_cols(cotangent, w_down))
    grad_pre_low = grad_pre.astype(jnp.bfloat16)
    grad_w_up = inner_rows(normed_two_low, grad_pre_low)
    grad_bias_up = jnp.sum(grad_pre_low.astype(jnp.float32), axis=0)
    grad_normed_two = lax.psum(inner_cols(grad_pre_low, w_up), "tensor")
    grad_hidden_part, grad_ln2_gain, grad_ln2_shift = norm_two_back(grad_normed_two)
    grad_hidden = grad_out + grad_hidden_part
    grad_ln2_gain, grad_ln2_shift, grad_w_up, grad_bias_up, grad_w_down, grad_bias_down = lax.psum(
        (grad_ln2_gain, grad_ln2_shift, grad_w_up, grad_bias_up, grad_w_down, grad_bias_down), "dp"
    )
    grad_hidden_low = grad_hidden.astype(jnp.bfloat16)
    grad_w_out = inner_rows(attended_low, grad_hidden_low)
    grad_bias_out = jnp.sum(grad_hidden, axis=0)
    grad_attended_low = inner_cols(grad_hidden_low, w_out).astype(jnp.bfloat16)
    block_count = 0
    seq_at = 0
    query_heads = heads_first(query, local_heads)
    key_heads = heads_first(keys, local_heads)
    value_heads = heads_first(values, local_heads)
    grad_heads = heads_first(grad_attended_low, local_heads)
    grad_key_heads = jnp.zeros(key_heads.shape, jnp.float32)
    grad_value_heads = jnp.zeros(value_heads.shape, jnp.float32)
    grad_query_blocks = []
    for start_row in range(0, seq_len, block_rows):
        query_block = query_heads[:, start_row : start_row + block_rows]
        grad_block = grad_heads[:, start_row : start_row + block_rows]
        scores = block_scores(query_block, key_heads, segments[seq_at], start_row, block_rows)
        chances_full = jnp.exp(scores - logsum_blocks[block_count])
        block_count = block_count + 1
        grad_chances = jnp.einsum(
            "hqd,hkd->hqk", grad_block, value_heads, preferred_element_type=jnp.float32
        )
        centre = jnp.sum(chances_full * grad_chances, axis=-1, keepdims=True)
        grad_scores = (chances_full * (grad_chances - centre)).astype(jnp.bfloat16)
        grad_query_blocks.append(
            jnp.einsum("hqk,hkd->hqd", grad_scores, key_heads, preferred_element_type=jnp.float32)
            * HD ** (-0.5)
        )
        grad_key_heads = grad_key_heads + jnp.einsum(
            "hqk,hqd->hkd", grad_scores, query_block, preferred_element_type=jnp.float32
        ) * HD ** (-0.5)
        grad_value_heads = grad_value_heads + jnp.einsum(
            "hqk,hqd->hkd",
            chances_full.astype(jnp.bfloat16),
            grad_block,
            preferred_element_type=jnp.float32,
        )
    grad_query_seqs = heads_last(jnp.concatenate(grad_query_blocks, axis=1))
    grad_key_seqs = heads_last(grad_key_heads)
    grad_value_seqs = heads_last(grad_value_heads)
    grad_query_low = grad_query_seqs.astype(jnp.bfloat16)
    grad_key_low = grad_key_seqs.astype(jnp.bfloat16)
    grad_value_low = grad_value_seqs.astype(jnp.bfloat16)
    grad_w_query = inner_rows(normed_low, grad_query_low)
    grad_bias_query = jnp.sum(grad_query_low.astype(jnp.float32), axis=0)
    grad_w_key = inner_rows(normed_low, grad_key_low)
    grad_w_value = inner_rows(normed_low, grad_value_low)
    grad_bias_value = jnp.sum(grad_value_low.astype(jnp.float32), axis=0)
    grad_normed_part = (
        inner_cols(grad_query_low, w_query)
        + inner_cols(grad_key_low, w_key)
        + inner_cols(grad_value_low, w_value)
    )
    grad_normed_one = lax.psum(grad_normed_part, "tensor")
    grad_input_part, grad_ln1_gain, grad_ln1_shift = norm_one_back(grad_normed_one)
    grad_input = grad_hidden + grad_input_part
    (
        grad_ln1_gain,
        grad_ln1_shift,
        grad_w_query,
        grad_bias_query,
        grad_w_key,
        grad_w_value,
        grad_bias_value,
        grad_w_out,
        grad_bias_out,
    ) = lax.psum(
        (
            grad_ln1_gain,
            grad_ln1_shift,
            grad_w_query,
            grad_bias_query,
            grad_w_key,
            grad_w_value,
            grad_bias_value,
            grad_w_out,
            grad_bias_out,
        ),
        "dp",
    )
    return (
        output,
        grad_input,
        grad_ln1_gain,
        grad_ln1_shift,
        grad_w_query,
        grad_bias_query,
        grad_w_key,
        grad_w_value,
        grad_bias_value,
        grad_w_out,
        grad_bias_out,
        grad_ln2_gain,
        grad_ln2_shift,
        grad_w_up,
        grad_bias_up,
        grad_w_down,
        grad_bias_down,
    )


def solution(mesh):
    in_specs = (
        P("dp", None),
        P("dp", None),
        P(),
        P(),
        P(None, "tensor"),
        P("tensor"),
        P(None, "tensor"),
        P(None, "tensor"),
        P("tensor"),
        P("tensor", None),
        P(),
        P(),
        P(),
        P(None, "tensor"),
        P("tensor"),
        P("tensor", None),
        P(),
        P("dp", None),
    )
    out_specs = (
        P("dp", None),
        P("dp", None),
        P(),
        P(),
        P(None, "tensor"),
        P("tensor"),
        P(None, "tensor"),
        P(None, "tensor"),
        P("tensor"),
        P("tensor", None),
        P(),
        P(),
        P(),
        P(None, "tensor"),
        P("tensor"),
        P("tensor", None),
        P(),
    )
    return jax.shard_map(
        per_device, mesh=mesh, in_specs=in_specs, out_specs=out_specs, check_vma=False
    )
```

profile of v0, /device:TPU:0, one launch (start us, length us, event | category | flops | bytes accessed | tf_op | source)
XLA Modules:
  0.0 670.6 jit_solution(14278935907362191674)
XLA Ops:
  7.3 1.8 convert_reduce_fusion
  9.2 2.1 fusion.20
  11.3 0.6 fusion.11
  12.0 0.7 convolution_convert_fusion.1
  12.7 0.7 fusion.41
  13.4 1.1 fusion.31
  14.5 1.4 fusion.72
  16.0 1.4 fusion.71
  17.5 1.5 fusion
  19.0 0.7 fusion.42
  19.7 1.7 fusion.44
  21.4 1.5 fusion.1
  22.9 1.7 fusion.43
  24.7 2.3 fusion.73
  27.2 123.7 %all-reduce.8.cloned.1.call-done = f32[1024,768]{1,0:T(8,128)} async-done(((f32[1024,768]{1,0:T(8,128)}), f32[1024,768]{1,0:T(8,128)}) %all-reduce.8.cloned.1.call-update) | async-done | bytes 3145744 | tf_op jit(solution)/shard_map/psum | solution.py:112
  150.9 2.4 fusion.68
  154.1 0.5 add_convert_fusion.1
  155.0 0.8 copy-done.59
  155.7 1.4 fusion.74
  157.7 4.3 convert_reduce_fusion.2
  162.0 1.2 copy-done.66
  163.2 3.1 fusion.75
  166.4 1.3 log_add_fusion
  167.7 0.7 log_add_fusion.1
  168.4 5.6 fusion.63
  174.1 112.5 %all-reduce.10.cloned.1.call-done = f32[1024,768]{1,0:T(8,128)} async-done(((f32[1024,768]{1,0:T(8,128)}), f32[1024,768]{1,0:T(8,128)}) %all-reduce.10.cloned.1.call-update) | async-done | bytes 3145744 | tf_op jit(solution)/shard_map/psum | solution.py:128
  286.6 4.7 multiply_reduce_fusion.2
  291.4 1.5 fusion.67
  292.9 0.8 convolution_convert_fusion
  293.7 0.9 copy-done.7
  294.6 1.2 slice-done.3
  295.8 1.2 fusion.23
  297.0 1.9 multiply_reduce_fusion
  299.0 1.9 multiply_reduce_fusion.1
  300.9 1.4 multiply_convert_fusion.1
  302.3 0.7 fusion.56
  303.0 1.1 convolution_multiply_fusion.1
  304.1 1.8 convert_reduce_fusion.3
  305.9 1.4 multiply_convert_fusion
  307.3 1.1 convolution_multiply_fusion
  308.4 0.7 fusion.37
  309.4 0.6 fusion.77
  310.2 0.6 fusion.76
  311.0 2.4 add_add_fusion.3
  313.7 5.0 fusion.78
  318.8 3.4 fusion.62
  322.1 1.3 fusion.81
  323.4 1.3 fusion.80
  324.8 1.3 fusion.79
  326.1 1.6 fusion.45
  327.7 0.6 copy-done.53
  328.5 207.2 %all-reduce.14.cloned.1.call-done = (f32[1024,768]{1,0:T(8,128)}, f32[1024,768]{1,0:T(8,128)}) async-done(((f32[1024,768]{1,0:T(8,128)}, f32[1024,768]{1,0:T(8,128)}), (f32[1024,768]{1,0:T(8,128)}, f32[1024,768]{1,0:T(8,128)})) %all-reduce.14.cloned.1.call-update) | async-done | bytes 6291472 | tf_op jit(solution)/shard_map/psum | solution.py:119
  535.8 2.9 fusion.65
  538.7 1.7 fusion.12
  541.0 2.9 convert_reduce_fusion.1
  543.9 26.0 %all-reduce = (f32[768]{0:T(1024)}, f32[768]{0:T(1024)}, f32[192]{0:T(256)}, f32[192]{0:T(256)}, f32[768]{0:T(1024)}, /*index=5*/f32[768]{0:T(1024)}, f32[768]{0:T(1024)}, f32[768]{0:T(1024)}, f32[768]{0:T(1024)}) all-reduce(f32[768]{0:T(1024)S(1)} %get-tuple-element.19, ...), channel_id=1, replica_groups=mesh['dp'=8,'tensor'=4] {'dp'}, use_global_device_ids=true, to_apply=%region_19.20 | all-reduce | flops 5760 | bytes 46080 | tf_op jit(solution)/shard_map/psum | solution.py:200
  569.9 4.6 add_convert_fusion
  574.5 79.6 %all-reduce.12.cloned.1.call-done = (f32[768,192]{0,1:T(8,128)}, f32[768,192]{0,1:T(8,128)}, f32[768,192]{0,1:T(8,128)}, f32[192,768]{1,0:T(8,128)}, f32[768,768]{1,0:T(8,128)}, /*index=5*/f32[768,768]{1,0:T(8,128)}) async-done(((f32[768,192]{0,1:T(8,128)}, f32[768,192]{0,1:T(8,128)}, f32[768,192]{0,1:T(8,128)}, f32[192,768]{1,0:T(8,128)}, f32[768,768]{1,0:T(8,128)}, /*index=5*/f32[768,768]{1,0:T(8,128)}), ...) | async-done | bytes 7077904 | tf_op jit(solution)/shard_map/psum | solution.py:200
  654.1 2.1 copy.45
  656.2 1.9 copy.46
  658.1 1.9 copy.47
  660.0 0.8 copy.48
  660.8 1.4 copy.49
  662.2 1.4 copy.50
  (162 shorter events, 4.0 us)
Async XLA Ops:
  7.2 150.0 %copy-start = (bf16[768,768]{1,0:T(8,128)(2,1)S(1)}, bf16[768,768]{1,0:T(8,128)(2,1)}, u32[]{:S(2)}) copy-start(bf16[768,768]{1,0:T(8,128)(2,1)} %param.33) | copy-start | bytes 3538948
  7.2 4.1 copy-start.6
  7.2 4.1 copy-start.52
  7.2 4.1 copy-start.36
  7.2 4.1 copy-start.55
  7.2 143.7 %all-reduce.8.cloned.1.call-start = ((), (), s32[]{:S(2)}) async-start(), calls=%async_computation | async-start | bytes 6291456 | tf_op jit(solution)/shard_map/psum | solution.py:112
  7.3 4.7 copy-start.30
  9.2 3.5 copy-start.32
  9.2 3.5 copy-start.62
  11.2 2.1 copy-start.44
  11.3 2.1 copy-start.38
  12.0 7.0 %copy-start.11 = (bf16[1024,768]{1,0:T(8,128)(2,1)}, bf16[1024,768]{1,0:T(8,128)(2,1)S(1)}, u32[]{:S(2)}) copy-start(bf16[1024,768]{1,0:T(8,128)(2,1)S(1)} %fusion.11) | copy-start | bytes 4718596
  13.4 2.6 copy-start.22
  16.0 3.7 copy-start.2
  16.0 3.7 copy-start.35
  17.4 5.5 copy-start.3
  17.4 1.5 copy-start.28
  19.0 2.4 copy-start.48
  19.7 3.2 copy-start.20
  22.9 1.7 copy-start.49
  22.9 1.7 copy-start.25
  24.7 126.3 %copy-start.56 = (f32[768]{0:T(1024)S(1)}, f32[768]{0:T(1024)}, u32[]{:S(2)}) copy-start(f32[768]{0:T(1024)} %param.28) | copy-start | bytes 9220
  27.0 259.6 %all-reduce.10.cloned.1.call-start = ((), (), s32[]{:S(2)}) async-start(), calls=%async_computation.1 | async-start | bytes 6291456 | tf_op jit(solution)/shard_map/psum | solution.py:128
  153.3 1.6 copy-start.4
  153.9 3.3 copy-start.46
  153.9 1.9 copy-start.59
  154.1 3.0 copy-start.40
  155.7 2.0 copy-start.13
  155.7 2.0 copy-start.60
  157.7 4.3 copy-start.64
  166.4 369.4 %all-reduce.14.cloned.1.call-start = ((), (), s32[]{:S(2)}) async-start(), calls=%async_computation.3 | async-start | bytes 12582912 | tf_op jit(solution)/shard_map/psum | solution.py:119
  174.1 117.2 %copy-start.47 = (f32[1024]{0:T(1024)S(1)}, f32[1024]{0:T(1024)}, u32[]{:S(2)}) copy-start(f32[1024]{0:T(1024)} %copy-done.46) | copy-start | bytes 12292
  174.1 117.2 %copy-start.41 = (f32[1024]{0:T(1024)S(1)}, f32[1024]{0:T(1024)}, u32[]{:S(2)}) copy-start(f32[1024]{0:T(1024)} %copy-done.40) | copy-start | bytes 12292
  174.1 117.3 %copy-start.43 = (f32[768]{0:T(1024)S(1)}, f32[768]{0:T(1024)}, u32[]{:S(2)}) copy-start(f32[768]{0:T(1024)} %param.29) | copy-start | bytes 9220
  286.6 4.7 copy-start.5
  286.6 4.7 copy-start.17
  291.3 3.3 slice-start.2
  291.3 1.6 copy-start.14
  291.4 1.6 copy-start.26
  291.4 4.4 slice-start.3
  292.9 1.7 copy-start.7
  292.9 2.9 copy-start.34
  295.8 3.1 slice-start
  297.0 2.0 slice-start.1
  313.4 5.4 copy-start.61
  313.4 340.7 %all-reduce.12.cloned.1.call-start = ((), (), s32[]{:S(2)}) async-start(), calls=%async_computation.2 | async-start | bytes 14155776 | tf_op jit(solution)/shard_map/psum | solution.py:200
  313.7 5.1 copy-start.15
  313.7 5.1 copy-start.65
  318.8 3.4 copy-start.12
  323.4 2.6 copy-start.8
  327.7 208.1 %copy-start.37 = (f32[768]{0:T(1024)S(1)}, f32[768]{0:T(1024)}, u32[]{:S(2)}) copy-start(f32[768]{0:T(1024)} %param.20) | copy-start | bytes 9220
  327.7 211.0 %copy-start.45 = (f32[1024]{0:T(1024)S(1)}, f32[1024]{0:T(1024)}, u32[]{:S(2)}) copy-start(f32[1024]{0:T(1024)} %copy-done.44) | copy-start | bytes 12292
  327.7 211.0 %copy-start.39 = (f32[1024]{0:T(1024)S(1)}, f32[1024]{0:T(1024)}, u32[]{:S(2)}) copy-start(f32[1024]{0:T(1024)} %copy-done.38) | copy-start | bytes 12292
  535.8 3.0 copy-start.10
  538.7 1.9 copy-start.9
  538.7 2.3 copy-start.16
  541.0 2.9 copy-start.50
  541.0 2.9 copy-start.51
  541.0 2.9 copy-start.58
  541.0 28.9 %copy-start.54 = (f32[768]{0:T(1024)S(1)}, f32[768]{0:T(1024)}, u32[]{:S(2)}) copy-start(f32[768]{0:T(1024)} %param.34) | copy-start | bytes 9220
  654.1 5.9 copy-start.27
  654.1 6.7 %copy-start.19 = (f32[768,768]{1,0:T(8,128)S(1)}, f32[768,768]{1,0:T(8,128)}, u32[]{:S(2)}) copy-start(f32[768,768]{1,0:T(8,128)} %get-tuple-element.79) | copy-start | bytes 7077892
  660.0 2.2 copy-start.18
  660.8 2.8 copy-start.1
  (11 other events, 11.9 us)
Sparse Core Ops, SparseCore 0:
  27.1 123.7 all-reduce.7
  166.5 120.0 all-reduce.9
  313.5 222.2 all-reduce.13
  540.8 113.2 all-reduce.11
where the time goes:
time: 679 us; the launch traced here: 671 us
  waiting for transfers between devices  523 us (77%)
  matrix products  53.6 us (8%)
  other arithmetic  35.3 us (5%)
  blocking collectives  26 us (4%)
  local copies, waits for them, and re-layouts  16.8 us (2%)
  between operations  15.1 us (2%)
    psum x1, waiting for transfers between devices, per_device(): feed_total = lax.psum(matmul(activated_low, w_down), 'tensor')  207 us
    psum x1, waiting for transfers between devices, per_device(): attention_total = lax.psum(matmul(attended_low, w_out), 'tensor')  124 us
    psum x1, waiting for transfers between devices, per_device(): grad_normed_two = lax.psum(inner_cols(grad_pre_low, w_up), 'tensor')  113 us
    psum x1, waiting for transfers between devices, per_device(): lax.psum((grad_ln1_gain, grad_ln1_shift, grad_w_query, grad_bias_query, g...  79.6 us
    psum x1, blocking collectives, per_device(): lax.psum((grad_ln1_gain, grad_ln1_shift, grad_w_query, grad_bias_query, g...  26 us
    unnamed x148, local copies, waits for them, and re-layouts  16.7 us
    dot_general x6, matrix products, inner_rows(): lax.dot_general(left_side, right_side, (((0,), (0,)), ((), ())), preferre...  13.9 us
  transfers between devices with their start and end apart: 4, of which 4 were waited for; matrix products, arithmetic and copies ran while one was open for 5% of the time, Pallas kernels for 0%

commit v1 on v0

--- a/solution.py
+++ b/solution.py
@@ -54,6 +54,86 @@
         "hqd,hkd->hqk", query_block, key_heads, preferred_element_type=jnp.float32
     ) * HD ** (-0.5)
     return jnp.where(allowed[None], scores, NEGATIVE)
+
+
+def swap(values, axis, bit):
+    return lax.ppermute(values, axis, [(i, i ^ bit) for i in range(lax.axis_size(axis))])
+
+
+def bits_of(axis):
+    return [1 << i for i in range(lax.axis_size(axis).bit_length() - 1)]
+
+
+def sum_scatter(values, axis, bits):
+    me = lax.axis_index(axis)
+    for bit in bits:
+        half = values.shape[0] // 2
+        mine = jnp.where(me & bit, 1, 0)
+        sent = lax.dynamic_slice_in_dim(values, (1 - mine) * half, half, 0)
+        values = lax.dynamic_slice_in_dim(values, mine * half, half, 0) + swap(sent, axis, bit)
+    return values
+
+
+def join(values, axis, bits):
+    me = lax.axis_index(axis)
+    for bit in reversed(bits):
+        other = swap(values, axis, bit)
+        upper = (me & bit) != 0
+        values = jnp.concatenate(
+            [jnp.where(upper, other, values), jnp.where(upper, values, other)], axis=0
+        )
+    return values
+
+
+def sum_all(values, axis, bits):
+    return join(sum_scatter(values, axis, bits), axis, bits)
+
+
+def sum_dp(values):
+    near, far = bits_of("dp")[:1], bits_of("dp")[1:]
+    cut = values.shape[1] // 2
+    first = sum_all(values[:, :cut], "dp", near + far)
+    second = sum_all(values[:, cut:], "dp", near + far[::-1])
+    return jnp.concatenate([first, second], axis=1)
+
+
+def sum_tensor(values, parts):
+    rows = values.shape[0] // parts
+    pieces = [values[i * rows : (i + 1) * rows] for i in range(parts)]
+    return jnp.concatenate([sum_all(p, "tensor", bits_of("tensor")) for p in pieces], axis=0)
+
+
+def spread(values, bits):
+    for bit in bits:
+        values = jnp.concatenate([values, swap(values, "dp", bit)], axis=0)
+    return values
+
+
+def rows_of(*vectors):
+    pad = jnp.zeros((64 - len(vectors), vectors[0].shape[0]), jnp.float32)
+    return jnp.concatenate([jnp.stack(vectors), pad], axis=0)
+
+
+def other_units(w_up, w_down, bias_up):
+    size, place = lax.axis_size("dp"), lax.axis_index("dp")
+    count = w_down.shape[0] // size
+    up_piece = lax.dynamic_slice_in_dim(w_up, place * count, count, 1).T.astype(jnp.float32) * 2.0
+    down_piece = lax.dynamic_slice_in_dim(w_down, place * count, count, 0).astype(jnp.float32) * 2.0
+    near, far = bits_of("dp")[:1], bits_of("dp")[1:]
+    first, second = far + near, far[::-1] + near
+    biases = lax.all_gather(bias_up, "tensor").reshape(-1, size, count)
+    me = lax.axis_index("tensor")
+    found = []
+    for offset in range(1, lax.axis_size("tensor")):
+        up_own, down_own = swap(up_piece, "tensor", offset), swap(down_piece, "tensor", offset)
+        bias = lax.dynamic_index_in_dim(biases, me ^ offset, 0, False)
+        order = jnp.arange(1) ^ place
+        for bit in first:
+            order = jnp.concatenate([order, order ^ bit])
+        ups, downs = spread(up_own, first), spread(down_own, first)
+        first, second = second, first
+        found.append((ups, downs, bias[order].reshape(-1)))
+    return found
 
 
 def per_device(
@@ -77,6 +157,7 @@
     cotangent,
 ):
     inputs = tokens_in.astype(jnp.float32)
+    others = other_units(w_up, w_down, bias_up)
     local_heads = w_query.shape[1] // HD
     seq_count, seq_len = segments.shape
     block_rows = min(512, seq_len)
@@ -109,28 +190,48 @@
         logsum_blocks.append(row_top + jnp.log(row_total))
     attended_seqs = heads_last(jnp.concatenate(mixed_blocks, axis=1))
     attended_low = attended_seqs.astype(jnp.bfloat16)
-    attention_total = lax.psum(matmul(attended_low, w_out), "tensor")
+    attention_total = sum_tensor(matmul(attended_low, w_out), 4)
     hidden_one = inputs + attention_total + bias_out
     normed_two, norm_two_back = jax.vjp(layer_norm, hidden_one, ln2_gain, ln2_shift)
     normed_two_low = normed_two.astype(jnp.bfloat16)
+    grad_out = cotangent.astype(jnp.float32)
     pre_act = matmul(normed_two_low, w_up) + bias_up
     activated, act_back = jax.vjp(smooth_unit, pre_act)
     activated_low = activated.astype(jnp.bfloat16)
-    feed_total = lax.psum(matmul(activated_low, w_down), "tensor")
-    output = (hidden_one + feed_total + bias_down).astype(jnp.bfloat16)
-    grad_out = cotangent.astype(jnp.float32)
+    feed_total = matmul(activated_low, w_down)
     grad_w_down = inner_rows(activated_low, cotangent)
     grad_bias_down = jnp.sum(grad_out, axis=0)
     (grad_pre,) = act_back(inner_cols(cotangent, w_down))
     grad_pre_low = grad_pre.astype(jnp.bfloat16)
     grad_w_up = inner_rows(normed_two_low, grad_pre_low)
     grad_bias_up = jnp.sum(grad_pre_low.astype(jnp.float32), axis=0)
-    grad_normed_two = lax.psum(inner_cols(grad_pre_low, w_up), "tensor")
+    grad_normed_two = inner_cols(grad_pre_low, w_up)
+    for up_part, down_part, bias_part in others:
+        up_part, down_part = (up_part * 0.5).astype(jnp.bfloat16), (down_part * 0.5).astype(jnp.bfloat16)
+        pre_act = inner_cols(normed_two_low, up_part) + bias_part
+        activated, act_back = jax.vjp(smooth_unit, pre_act)
+        feed_total = feed_total + matmul(activated.astype(jnp.bfloat16), down_part)
+        (grad_pre,) = act_back(inner_cols(cotangent, down_part))
+        grad_normed_two = grad_normed_two + matmul(grad_pre.astype(jnp.bfloat16), up_part)
+    output = (hidden_one + feed_total + bias_down).astype(jnp.bfloat16)
     grad_hidden_part, grad_ln2_gain, grad_ln2_shift = norm_two_back(grad_normed_two)
     grad_hidden = grad_out + grad_hidden_part
-    grad_ln2_gain, grad_ln2_shift, grad_w_up, grad_bias_up, grad_w_down, grad_bias_down = lax.psum(
-        (grad_ln2_gain, grad_ln2_shift, grad_w_up, grad_bias_up, grad_w_down, grad_bias_down), "dp"
-    )
+    units = w_up.shape[1]
+    total = sum_dp(
+        jnp.concatenate(
+            [
+                grad_w_up,
+                grad_w_down,
+                rows_of(grad_ln2_gain, grad_ln2_shift, grad_bias_up, grad_bias_down),
+            ],
+            axis=0,
+        )
+    )
+    width = w_up.shape[0]
+    grad_w_up, grad_w_down = total[:width], total[width : width + units]
+    grad_ln2_gain, grad_ln2_shift, grad_bias_up, grad_bias_down = total[
+        width + units : width + units + 4
+    ]
     grad_hidden_low = grad_hidden.astype(jnp.bfloat16)
     grad_w_out = inner_rows(attended_low, grad_hidden_low)
     grad_bias_out = jnp.sum(grad_hidden, axis=0)
@@ -174,43 +275,41 @@
     grad_query_low = grad_query_seqs.astype(jnp.bfloat16)
     grad_key_low = grad_key_seqs.astype(jnp.bfloat16)
     grad_value_low = grad_value_seqs.astype(jnp.bfloat16)
-    grad_w_query = inner_rows(normed_low, grad_query_low)
-    grad_bias_query = jnp.sum(grad_query_low.astype(jnp.float32), axis=0)
-    grad_w_key = inner_rows(normed_low, grad_key_low)
-    grad_w_value = inner_rows(normed_low, grad_value_low)
-    grad_bias_value = jnp.sum(grad_value_low.astype(jnp.float32), axis=0)
     grad_normed_part = (
         inner_cols(grad_query_low, w_query)
         + inner_cols(grad_key_low, w_key)
         + inner_cols(grad_value_low, w_value)
     )
-    grad_normed_one = lax.psum(grad_normed_part, "tensor")
-    grad_input_part, grad_ln1_gain, grad_ln1_shift = norm_one_back(grad_normed_one)
+    grad_normed_one = sum_tensor(grad_normed_part, 4)
+    grad_bias_query = jnp.sum(grad_query_low.astype(jnp.float32), axis=0)
+    grad_bias_value = jnp.sum(grad_value_low.astype(jnp.float32), axis=0)
+    _, grad_ln1_gain, grad_ln1_shift = norm_one_back(grad_normed_part)
+    held = w_query.shape[1]
+    width = w_query.shape[0]
+    head_bias = jnp.zeros((width,), jnp.float32)
+    head_bias = head_bias.at[:held].set(grad_bias_query).at[held : 2 * held].set(grad_bias_value)
+    total = sum_dp(
+        jnp.concatenate(
+            [
+                inner_rows(grad_query_low, normed_low),
+                inner_rows(grad_key_low, normed_low),
+                inner_rows(grad_value_low, normed_low),
+                grad_w_out,
+                rows_of(grad_ln1_gain, grad_ln1_shift, grad_bias_out, head_bias),
+            ],
+            axis=0,
+        )
+    )
+    grad_w_query = total[:held].T
+    grad_w_key = total[held : 2 * held].T
+    grad_w_value = total[2 * held : 3 * held].T
+    grad_w_out = total[3 * held : 4 * held]
+    grad_ln1_gain, grad_ln1_shift = lax.psum(total[4 * held : 4 * held + 2], "tensor")
+    grad_bias_out = total[4 * held + 2]
+    grad_bias_query = total[4 * held + 3, :held]
+    grad_bias_value = total[4 * held + 3, held : 2 * held]
+    grad_input_part, _, _ = norm_one_back(grad_normed_one)
     grad_input = grad_hidden + grad_input_part
-    (
-        grad_ln1_gain,
-        grad_ln1_shift,
-        grad_w_query,
-        grad_bias_query,
-        grad_w_key,
-        grad_w_value,
-        grad_bias_value,
-        grad_w_out,
-        grad_bias_out,
-    ) = lax.psum(
-        (
-            grad_ln1_gain,
-            grad_ln1_shift,
-            grad_w_query,
-            grad_bias_query,
-            grad_w_key,
-            grad_w_value,
-            grad_bias_value,
-            grad_w_out,
-            grad_bias_out,
-        ),
-        "dp",
-    )
     return (
         output,
         grad_input,

time: 679 us -> 608 us (0.90)
  waiting for transfers between devices: 523 us -> 272 us
  starting transfers between devices: 0.59 us -> 67.5 us
  matrix products: 53.6 us -> 105 us
  local copies, waits for them, and re-layouts: 16.8 us -> 57.9 us
  other arithmetic: 35.3 us -> 61.1 us
  between operations: 15.1 us -> 3.26 us
    psum x4 -> x0, waiting for transfers between devices: 523 us -> none  [the longest x1 207 us: per_device(): feed_total = lax.psum(matmul(activated_low, w_down), 'tensor')]
    ppermute x0 -> x80, waiting for transfers between devices: none -> 272 us  [swap(): lax.ppermute(values, axis, [(i, i ^ bit) for i in range(lax.axis_size(axi...]
    ppermute x0 -> x80, starting transfers between devices: none -> 67.5 us  [swap(): lax.ppermute(values, axis, [(i, i ^ bit) for i in range(lax.axis_size(axi...]
    dot_general x6 -> x12, matrix products: 11.3 us -> 52.5 us  [matmul(): return jnp.dot(left_side, right_side, preferred_element_type=jnp.float32)]
    all_gather x0 -> x1, blocking collectives: none -> 21.6 us  [other_units(): biases = lax.all_gather(bias_up, 'tensor').reshape(-1, size, count)]
    concatenate x0 -> x2, local copies, waits for them, and re-layouts: none -> 18.4 us  [the longest x1 12.2 us: per_device(): jnp.concatenate([grad_w_up, grad_w_down, rows_of(grad_ln2_gain, grad_ln2_...]
    psum x1, blocking collectives: 26 us -> 9.52 us  [per_device(): lax.psum(total[4 * held:4 * held + 2], 'tensor')]
    concatenate x0 -> x36, other arithmetic: none -> 14.3 us  [the longest x12 7.63 us: spread(): values = jnp.concatenate([values, swap(values, 'dp', bit)], axis=0)]
  transfers between devices with their start and end apart: 4 -> 80, of which waited for: 4 -> 31; matrix products, arithmetic and copies ran while one was open for 5% -> 26% of each run, Pallas kernels for 0% -> 0%
where the time goes in v1:
time: 608 us; the launch traced here: 598 us
  waiting for transfers between devices  272 us (45%)
  matrix products  105 us (17%)
  starting transfers between devices  67.5 us (11%)
  other arithmetic  61.1 us (10%)
  local copies, waits for them, and re-layouts  57.9 us (10%)
  blocking collectives  31.1 us (5%)
    ppermute x80, waiting for transfers between devices, swap(): lax.ppermute(values, axis, [(i, i ^ bit) for i in range(lax.axis_size(axi...  272 us
    ppermute x80, starting transfers between devices, swap(): lax.ppermute(values, axis, [(i, i ^ bit) for i in range(lax.axis_size(axi...  67.5 us
    dot_general x12, matrix products, matmul(): return jnp.dot(left_side, right_side, preferred_element_type=jnp.float32)  52.5 us
    dot_general x9, matrix products, inner_cols(): lax.dot_general(left_side, right_side, (((1,), (1,)), ((), ())), preferre...  23.7 us
    all_gather x1, blocking collectives, other_units(): biases = lax.all_gather(bias_up, 'tensor').reshape(-1, size, count)  21.6 us
    concatenate x1, local copies, waits for them, and re-layouts, per_device(): jnp.concatenate([grad_w_up, grad_w_down, rows_of(grad_ln2_gain, grad_ln2_...  12.2 us
  transfers between devices with their start and end apart: 80, of which 31 were waited for; matrix products, arithmetic and copies ran while one was open for 26% of the time, Pallas kernels for 0%

profile of v1, /device:TPU:0, one launch (start us, length us, event | category | flops | bytes accessed | tf_op | source)
XLA Modules:
  0.0 597.7 jit_solution(13194382792998639449)
XLA Ops:
  2.9 3.0 collective-permute-start.16
  6.0 2.6 collective-permute-start.24
  27.2 1.8 constant_dynamic-slice_fusion.25
  29.5 1.8 constant_dynamic-slice_fusion.27
  32.8 1.8 constant_dynamic-slice_fusion.29
  42.6 21.6 %all-gather.1 = f32[4,1,768]{2,1,0:T(1,128)} all-gather(f32[1,1,768]{2,1,0:T(1,128)S(1)} %reshape.811), channel_id=2, replica_groups=mesh['dp'=8,'tensor'=4] {'tensor'}, dimensions={0}, use_global_device_ids=true | all-gather | bytes 15360 | tf_op jit(solution)/shard_map/all_gather | solution.py:124
  76.4 2.0 collective-permute-start.20
  81.3 13.0 %collective-permute-done = f32[128,768]{1,0:T(8,128)S(1)} collective-permute-done((f32[128,768]{1,0:T(8,128)S(1)}, f32[128,768]{1,0:T(8,128)S(1)}, u32[]{:S(2)}, u32[]{:S(2)}) %collective-permute-start) | collective-permute-done | bytes 393248 | tf_op jit(solution)/shard_map/ppermute | solution.py:60
  94.4 11.5 %collective-permute-done.13 = f32[64,768]{1,0:T(8,128)S(1)} collective-permute-done((f32[64,768]{1,0:T(8,128)S(1)}, f32[64,768]{1,0:T(8,128)S(1)}, u32[]{:S(2)}, u32[]{:S(2)}) %collective-permute-start.13) | collective-permute-done | bytes 196640 | tf_op jit(solution)/shard_map/ppermute | solution.py:60
  106.0 17.8 %collective-permute-done.9 = f32[64,768]{1,0:T(8,128)S(1)} collective-permute-done((f32[64,768]{1,0:T(8,128)S(1)}, f32[64,768]{1,0:T(8,128)S(1)}, u32[]{:S(2)}, u32[]{:S(2)}) %collective-permute-start.9) | collective-permute-done | bytes 196640 | tf_op jit(solution)/shard_map/ppermute | solution.py:60
  125.4 2.2 collective-permute-start.36
  129.1 11.8 %collective-permute-done.5 = f32[64,768]{1,0:T(8,128)S(1)} collective-permute-done((f32[64,768]{1,0:T(8,128)S(1)}, f32[64,768]{1,0:T(8,128)S(1)}, u32[]{:S(2)}, u32[]{:S(2)}) %collective-permute-start.5) | collective-permute-done | bytes 196640 | tf_op jit(solution)/shard_map/ppermute | solution.py:60
  142.6 12.6 %collective-permute-done.1 = f32[64,768]{1,0:T(8,128)S(1)} collective-permute-done((f32[64,768]{1,0:T(8,128)S(1)}, f32[64,768]{1,0:T(8,128)S(1)}, u32[]{:S(2)}, u32[]{:S(2)}) %collective-permute-start.1) | collective-permute-done | bytes 196640 | tf_op jit(solution)/shard_map/ppermute | solution.py:60
  160.5 2.0 collective-permute-done.25
  166.7 2.7 collective-permute-start.2
  171.1 18.9 %collective-permute-done.2 = f32[64,768]{1,0:T(8,128)S(1)} collective-permute-done((f32[64,768]{1,0:T(8,128)S(1)}, f32[64,768]{1,0:T(8,128)S(1)}, u32[]{:S(2)}, u32[]{:S(2)}) %collective-permute-start.2) | collective-permute-done | bytes 196640 | tf_op jit(solution)/shard_map/ppermute | solution.py:60
  194.1 8.7 %collective-permute-done.3 = f32[128,768]{1,0:T(8,128)S(1)} collective-permute-done((f32[128,768]{1,0:T(8,128)S(1)}, f32[128,768]{1,0:T(8,128)S(1)}, u32[]{:S(2)}, u32[]{:S(2)}) %collective-permute-start.3) | collective-permute-done | bytes 393248 | tf_op jit(solution)/shard_map/ppermute | solution.py:60
  203.1 8.9 %collective-permute-done.7 = f32[128,768]{1,0:T(8,128)S(1)} collective-permute-done((f32[128,768]{1,0:T(8,128)S(1)}, f32[128,768]{1,0:T(8,128)S(1)}, u32[]{:S(2)}, u32[]{:S(2)}) %collective-permute-start.7) | collective-permute-done | bytes 393248 | tf_op jit(solution)/shard_map/ppermute | solution.py:60
  212.4 8.8 %collective-permute-done.11 = f32[128,768]{1,0:T(8,128)S(1)} collective-permute-done((f32[128,768]{1,0:T(8,128)S(1)}, f32[128,768]{1,0:T(8,128)S(1)}, u32[]{:S(2)}, u32[]{:S(2)}) %collective-permute-start.11) | collective-permute-done | bytes 393248 | tf_op jit(solution)/shard_map/ppermute | solution.py:60
  221.7 7.3 %collective-permute-done.15 = f32[128,768]{1,0:T(8,128)S(1)} collective-permute-done((f32[128,768]{1,0:T(8,128)S(1)}, f32[128,768]{1,0:T(8,128)S(1)}, u32[]{:S(2)}, u32[]{:S(2)}) %collective-permute-start.15) | collective-permute-done | bytes 393248 | tf_op jit(solution)/shard_map/ppermute | solution.py:60
  235.9 4.2 convert_reduce_fusion.2
  240.3 3.3 fusion.161
  245.2 3.7 fusion.162
  251.7 3.2 fusion.183
  256.9 2.9 fusion.189
  260.1 4.1 fusion.158
  264.3 4.3 fusion.152
  268.7 9.3 %fusion.76 = f32[1024,768]{1,0:T(8,128)} fusion(f32[1024,768]{1,0:T(8,128)} %fusion.158, bf16[1024,768]{1,0:T(8,128)(2,1)} %param.39, f32[768]{0:T(1024)} %add.470, f32[384,768]{1,0:T(8,128)} %collective-permute-done.23, f32[192,768]{1,0:T(8,128)} %copy-done.66, f32[96,768]{1,0:T(8,128)S(1)} %copy-done.50, f32[96,768]{1,0:T(8,128)S(1)} %copy-done.41, ...), kind=kOutput, calls=%fused_computation.133 | convolution fusion | flops 2438332416 | bytes 12585984 | tf_op jit(solution)/shard_map/dot_general | solution.py:24
  278.0 5.2 fusion.146
  283.2 9.2 %fusion.75 = f32[1024,768]{1,0:T(8,128)} fusion(f32[1024,768]{1,0:T(8,128)} %fusion.152, bf16[1024,768]{1,0:T(8,128)(2,1)} %param.39, f32[768]{0:T(1024)} %add.478, f32[384,768]{1,0:T(8,128)} %collective-permute-done.31, f32[192,768]{1,0:T(8,128)} %copy-done.68, f32[96,768]{1,0:T(8,128)S(1)} %copy-done.53, f32[96,768]{1,0:T(8,128)S(1)} %copy-done.44, ...), kind=kOutput, calls=%fused_computation.132 | convolution fusion | flops 2438332416 | bytes 12585984 | tf_op jit(solution)/shard_map/dot_general | solution.py:24
  292.4 14.1 %multiply_reduce_fusion.2 = (f32[768]{0:T(1024)}, f32[1024]{0:T(1024)S(1)}, f32[768]{0:T(1024)}, f32[1024,768]{1,0:T(8,128)}) fusion(f32[1024,768]{1,0:T(8,128)} %copy-done.5, f32[1024]{0:T(1024)S(1)} %fusion.107, f32[1024]{0:T(1024)S(1)} %broadcast_multiply_fusion, f32[768]{0:T(1024)S(1)} %copy-done.95, f32[384,768]{1,0:T(8,128)} %collective-permute-done.35, ...), kind=kOutput, calls=%fused_computation.93 | convolution fusion | flops 2446980608 | bytes 25190400 | tf_op jit(solution)/shard_map/dot_general | solution.py:24
  306.6 3.7 fusion.166
  311.2 1.8 slice-done.3
  313.0 2.0 fusion.44
  315.0 1.9 multiply_reduce_fusion
  317.0 1.9 multiply_reduce_fusion.1
  323.8 1.8 multiply_convert_fusion
  340.1 3.6 fusion.73
  343.9 3.6 fusion.74
  348.3 5.0 add_convert_fusion
  362.9 10.7 %collective-permute-done.44 = f32[128,768]{1,0:T(8,128)} collective-permute-done((f32[128,768]{1,0:T(8,128)}, f32[128,768]{1,0:T(8,128)}, u32[]{:S(2)}, u32[]{:S(2)}) %collective-permute-start.44) | collective-permute-done | bytes 393248 | tf_op jit(solution)/shard_map/ppermute | solution.py:60
  375.7 5.8 collective-permute-done.40
  383.7 2.0 collective-permute-start.54
  386.8 16.9 %collective-permute-done.45 = f32[64,768]{1,0:T(8,128)S(1)} collective-permute-done((f32[64,768]{1,0:T(8,128)S(1)}, f32[64,768]{1,0:T(8,128)S(1)}, u32[]{:S(2)}, u32[]{:S(2)}) %collective-permute-start.45) | collective-permute-done | bytes 196640 | tf_op jit(solution)/shard_map/ppermute | solution.py:60
  403.8 8.3 %collective-permute-done.41 = f32[64,768]{1,0:T(8,128)S(1)} collective-permute-done((f32[64,768]{1,0:T(8,128)S(1)}, f32[64,768]{1,0:T(8,128)S(1)}, u32[]{:S(2)}, u32[]{:S(2)}) %collective-permute-start.41) | collective-permute-done | bytes 196640 | tf_op jit(solution)/shard_map/ppermute | solution.py:60
  412.2 8.3 %collective-permute-done.54 = f32[64,768]{1,0:T(8,128)S(1)} collective-permute-done((f32[64,768]{1,0:T(8,128)S(1)}, f32[64,768]{1,0:T(8,128)S(1)}, u32[]{:S(2)}, u32[]{:S(2)}) %collective-permute-start.54) | collective-permute-done | bytes 196640 | tf_op jit(solution)/shard_map/ppermute | solution.py:60
  420.7 12.5 %collective-permute-done.42 = f32[64,768]{1,0:T(8,128)S(1)} collective-permute-done((f32[64,768]{1,0:T(8,128)S(1)}, f32[64,768]{1,0:T(8,128)S(1)}, u32[]{:S(2)}, u32[]{:S(2)}) %collective-permute-start.42) | collective-permute-done | bytes 196640 | tf_op jit(solution)/shard_map/ppermute | solution.py:60
  433.4 2.1 collective-permute-start.51
  435.6 14.4 %collective-permute-done.43 = f32[128,768]{1,0:T(8,128)S(1)} collective-permute-done((f32[128,768]{1,0:T(8,128)S(1)}, f32[128,768]{1,0:T(8,128)S(1)}, u32[]{:S(2)}, u32[]{:S(2)}) %collective-permute-start.43) | collective-permute-done | bytes 393248 | tf_op jit(solution)/shard_map/ppermute | solution.py:60
  450.1 16.6 %collective-permute-done.47 = f32[128,768]{1,0:T(8,128)S(1)} collective-permute-done((f32[128,768]{1,0:T(8,128)S(1)}, f32[128,768]{1,0:T(8,128)S(1)}, u32[]{:S(2)}, u32[]{:S(2)}) %collective-permute-start.47) | collective-permute-done | bytes 393248 | tf_op jit(solution)/shard_map/ppermute | solution.py:60
  469.0 1.8 fusion.164
  471.4 2.8 convert_reduce_fusion.1
  474.2 6.2 %concatenate.325 = f32[832,768]{1,0:T(8,128)S(1)} concatenate(f32[192,768]{1,0:T(8,128)} %fusion.186, f32[192,768]{1,0:T(8,128)} %fusion.187, f32[192,768]{1,0:T(8,128)} %fusion.188, f32[192,768]{1,0:T(8,128)S(1)} %copy-done.33, f32[1,768]{1,0:T(1,128)S(1)} %reshape.781, f32[1,768]{1,0:T(1,128)S(1)} %reshape.782, f32[1,768]{1,0:T(1,128)S(1)} %stack.18, f32[1,768]{1,0:T(1,128)S(1)} %scatter.9, ...), dimensions={0} | concatenate | bytes 5111808 | tf_op jit(solution)/shard_map/concatenate | solution.py:292
  483.5 12.2 %concatenate.333 = f32[1600,768]{1,0:T(8,128)} concatenate(f32[768,768]{1,0:T(8,128)} %fusion.189, f32[768,768]{1,0:T(8,128)S(1)} %copy-done.34, f32[1,768]{1,0:T(1,128)S(1)} %reshape.783, f32[1,768]{1,0:T(1,128)S(1)} %reshape.784, f32[1,768]{1,0:T(1,128)S(1)} %copy-done.97, f32[1,768]{1,0:T(1,128)S(1)} %stack.22, f32[60,768]{1,0:T(8,128)S(1)} %broadcast.332), dimensions={0} | concatenate | bytes 9830400 | tf_op jit(solution)/shard_map/concatenate | solution.py:221
  495.7 2.8 fusion.170
  503.3 7.2 %collective-permute-done.57 = f32[208,384]{1,0:T(8,128)S(1)} collective-permute-done((f32[208,384]{1,0:T(8,128)S(1)}, f32[208,384]{1,0:T(8,128)S(1)}, u32[]{:S(2)}, u32[]{:S(2)}) %collective-permute-start.57) | collective-permute-done | bytes 319520 | tf_op jit(solution)/shard_map/ppermute | solution.py:60
  512.0 2.1 collective-permute-start.64
  517.4 2.1 collective-permute-start.65
  525.3 16.2 %collective-permute-done.60 = f32[208,384]{1,0:T(8,128)S(1)} collective-permute-done((f32[208,384]{1,0:T(8,128)S(1)}, f32[208,384]{1,0:T(8,128)S(1)}, u32[]{:S(2)}, u32[]{:S(2)}) %collective-permute-start.60) | collective-permute-done | bytes 319520 | tf_op jit(solution)/shard_map/ppermute | solution.py:60
  544.5 7.1 %collective-permute-done.70 = f32[200,384]{1,0:T(8,128)S(1)} collective-permute-done((f32[200,384]{1,0:T(8,128)S(1)}, f32[200,384]{1,0:T(8,128)S(1)}, u32[]{:S(2)}, u32[]{:S(2)}) %collective-permute-start.70) | collective-permute-done | bytes 307232 | tf_op jit(solution)/shard_map/ppermute | solution.py:60
  554.2 6.4 %collective-permute-done.71 = f32[200,384]{1,0:T(8,128)S(1)} collective-permute-done((f32[200,384]{1,0:T(8,128)S(1)}, f32[200,384]{1,0:T(8,128)S(1)}, u32[]{:S(2)}, u32[]{:S(2)}) %collective-permute-start.71) | collective-permute-done | bytes 307232 | tf_op jit(solution)/shard_map/ppermute | solution.py:60
  563.8 11.5 %collective-permute-done.72 = f32[400,384]{1,0:T(8,128)S(1)} collective-permute-done((f32[400,384]{1,0:T(8,128)S(1)}, f32[400,384]{1,0:T(8,128)S(1)}, u32[]{:S(2)}, u32[]{:S(2)}) %collective-permute-start.72) | collective-permute-done | bytes 614432 | tf_op jit(solution)/shard_map/ppermute | solution.py:60
  578.5 9.5 %psum.7 = f32[2,768]{1,0:T(2,128)S(1)} all-reduce(f32[2,768]{1,0:T(2,128)S(1)} %maximum_maximum_fusion.2), channel_id=1, replica_groups=mesh['dp'=8,'tensor'=4] {'tensor'}, use_global_device_ids=true, to_apply=%region_19.20 | all-reduce | flops 1536 | bytes 12288 | tf_op jit(solution)/shard_map/psum | solution.py:307
  595.1 2.5 fusion.169
  (579 shorter events, 156.7 us)
Async XLA Ops:
  2.9 120.8 %collective-permute-start.16 = (f32[96,768]{1,0:T(8,128)}, f32[96,768]{1,0:T(8,128)}, u32[]{:S(2)}, u32[]{:S(2)}) collective-permute-start(f32[96,768]{1,0:T(8,128)} %multiply_bitcast_fusion), channel_id=1, source_target_pairs={{0,1},{1,0},{2,3},{3,2},{4,5},{5,4},{6,7},{7,6},{8,9},{9,8},{10,11... | collective-permute-start | bytes 884744 | tf_op jit(solution)/shard_map/ppermute | solution.py:60
  6.0 121.7 %collective-permute-start.24 = (f32[96,768]{1,0:T(8,128)}, f32[96,768]{1,0:T(8,128)}, u32[]{:S(2)}, u32[]{:S(2)}) collective-permute-start(f32[96,768]{1,0:T(8,128)} %multiply_bitcast_fusion), channel_id=1, source_target_pairs={{0,2},{1,3},{2,0},{3,1},{4,6},{5,7},{6,4},{7,5},{8,10},{9,11},{10,... | collective-permute-start | bytes 884744 | tf_op jit(solution)/shard_map/ppermute | solution.py:60
  29.0 46.1 %collective-permute-start.12 = (f32[128,768]{1,0:T(8,128)}, f32[128,768]{1,0:T(8,128)}, u32[]{:S(2)}, u32[]{:S(2)}) collective-permute-start(f32[128,768]{1,0:T(8,128)} %constant_dynamic-slice_fusion.25), channel_id=1, source_target_pairs={{0,1},{1,0},{2,3},{3,2},{4,5},{5,4},{6,7},{7,6},{8,9},{9,8},{10,11... | collective-permute-start | bytes 1179656 | tf_op jit(solution)/shard_map/ppermute | solution.py:60
  31.2 45.2 %collective-permute-start.8 = (f32[128,768]{1,0:T(8,128)}, f32[128,768]{1,0:T(8,128)}, u32[]{:S(2)}, u32[]{:S(2)}) collective-permute-start(f32[128,768]{1,0:T(8,128)} %constant_dynamic-slice_fusion.27), channel_id=1, source_target_pairs={{0,1},{1,0},{2,3},{3,2},{4,5},{5,4},{6,7},{7,6},{8,9},{9,8},{10,11... | collective-permute-start | bytes 1179656 | tf_op jit(solution)/shard_map/ppermute | solution.py:60
  34.6 45.1 %collective-permute-start.4 = (f32[128,768]{1,0:T(8,128)}, f32[128,768]{1,0:T(8,128)}, u32[]{:S(2)}, u32[]{:S(2)}) collective-permute-start(f32[128,768]{1,0:T(8,128)} %constant_dynamic-slice_fusion.29), channel_id=1, source_target_pairs={{0,1},{1,0},{2,3},{3,2},{4,5},{5,4},{6,7},{7,6},{8,9},{9,8},{10,11... | collective-permute-start | bytes 1179656 | tf_op jit(solution)/shard_map/ppermute | solution.py:60
  75.1 19.2 %collective-permute-start = (f32[128,768]{1,0:T(8,128)S(1)}, f32[128,768]{1,0:T(8,128)S(1)}, u32[]{:S(2)}, u32[]{:S(2)}) collective-permute-start(f32[128,768]{1,0:T(8,128)S(1)} %constant_dynamic-slice_fusion.31), channel_id=1, source_target_pairs={{0,1},{1,0},{2,3},{3,2},{4,5},{5,4},{6,7},{7,6},{8,9},{9,8},{10,11... | collective-permute-start | bytes 1179656 | tf_op jit(solution)/shard_map/ppermute | solution.py:60
  76.4 49.0 %collective-permute-start.20 = (f32[96,768]{1,0:T(8,128)}, f32[96,768]{1,0:T(8,128)S(1)}, u32[]{:S(2)}, u32[]{:S(2)}) collective-permute-start(f32[96,768]{1,0:T(8,128)} %convert_multiply_fusion), channel_id=1, source_target_pairs={{0,1},{1,0},{2,3},{3,2},{4,5},{5,4},{6,7},{7,6},{8,9},{9,8},{10,11... | collective-permute-start | bytes 884744 | tf_op jit(solution)/shard_map/ppermute | solution.py:60
  79.7 61.3 %collective-permute-start.28 = (f32[96,768]{1,0:T(8,128)S(1)}, f32[96,768]{1,0:T(8,128)S(1)}, u32[]{:S(2)}, u32[]{:S(2)}) collective-permute-start(f32[96,768]{1,0:T(8,128)S(1)} %copy-done.77), channel_id=1, source_target_pairs={{0,2},{1,3},{2,0},{3,1},{4,6},{5,7},{6,4},{7,5},{8,10},{9,11},{10,... | collective-permute-start | bytes 884744 | tf_op jit(solution)/shard_map/ppermute | solution.py:60
  94.3 11.6 %collective-permute-start.13 = (f32[64,768]{1,0:T(8,128)S(1)}, f32[64,768]{1,0:T(8,128)S(1)}, u32[]{:S(2)}, u32[]{:S(2)}) collective-permute-start(f32[64,768]{1,0:T(8,128)S(1)} %constant_dynamic-slice_fusion.24), channel_id=1, source_target_pairs={{0,2},{1,3},{2,0},{3,1},{4,6},{5,7},{6,4},{7,5},{8,10},{9,11},{10,... | collective-permute-start | bytes 589832 | tf_op jit(solution)/shard_map/ppermute | solution.py:60
  105.9 17.8 %collective-permute-start.9 = (f32[64,768]{1,0:T(8,128)S(1)}, f32[64,768]{1,0:T(8,128)S(1)}, u32[]{:S(2)}, u32[]{:S(2)}) collective-permute-start(f32[64,768]{1,0:T(8,128)S(1)} %constant_dynamic-slice_fusion.26), channel_id=1, source_target_pairs={{0,2},{1,3},{2,0},{3,1},{4,6},{5,7},{6,4},{7,5},{8,10},{9,11},{10,... | collective-permute-start | bytes 589832 | tf_op jit(solution)/shard_map/ppermute | solution.py:60
  123.7 17.3 %collective-permute-start.5 = (f32[64,768]{1,0:T(8,128)S(1)}, f32[64,768]{1,0:T(8,128)S(1)}, u32[]{:S(2)}, u32[]{:S(2)}) collective-permute-start(f32[64,768]{1,0:T(8,128)S(1)} %constant_dynamic-slice_fusion.28), channel_id=1, source_target_pairs={{0,2},{1,3},{2,0},{3,1},{4,6},{5,7},{6,4},{7,5},{8,10},{9,11},{10,... | collective-permute-start | bytes 589832 | tf_op jit(solution)/shard_map/ppermute | solution.py:60
  123.8 33.0 %collective-permute-start.32 = (f32[96,768]{1,0:T(8,128)}, f32[96,768]{1,0:T(8,128)S(1)}, u32[]{:S(2)}, u32[]{:S(2)}) collective-permute-start(f32[96,768]{1,0:T(8,128)} %multiply_bitcast_fusion), channel_id=1, source_target_pairs={{0,3},{1,2},{2,1},{3,0},{4,7},{5,6},{6,5},{7,4},{8,11},{9,10},{10,... | collective-permute-start | bytes 884744 | tf_op jit(solution)/shard_map/ppermute | solution.py:60
  125.4 31.9 %collective-permute-start.36 = (f32[96,768]{1,0:T(8,128)S(1)}, f32[96,768]{1,0:T(8,128)S(1)}, u32[]{:S(2)}, u32[]{:S(2)}) collective-permute-start(f32[96,768]{1,0:T(8,128)S(1)} %copy-done.77), channel_id=1, source_target_pairs={{0,3},{1,2},{2,1},{3,0},{4,7},{5,6},{6,5},{7,4},{8,11},{9,10},{10,... | collective-permute-start | bytes 884744 | tf_op jit(solution)/shard_map/ppermute | solution.py:60
  127.6 31.2 %collective-permute-start.17 = (f32[96,768]{1,0:T(8,128)}, f32[96,768]{1,0:T(8,128)S(1)}, u32[]{:S(2)}, u32[]{:S(2)}) collective-permute-start(f32[96,768]{1,0:T(8,128)} %collective-permute-done.16), channel_id=1, source_target_pairs={{0,8},{4,12},{8,0},{12,4},{16,24},{20,28},{24,16},{28,20},{1,9},{5... | collective-permute-start | bytes 884744 | tf_op jit(solution)/shard_map/ppermute | solution.py:60
  141.0 14.2 %collective-permute-start.1 = (f32[64,768]{1,0:T(8,128)S(1)}, f32[64,768]{1,0:T(8,128)S(1)}, u32[]{:S(2)}, u32[]{:S(2)}) collective-permute-start(f32[64,768]{1,0:T(8,128)S(1)} %constant_dynamic-slice_fusion.30), channel_id=1, source_target_pairs={{0,2},{1,3},{2,0},{3,1},{4,6},{5,7},{6,4},{7,5},{8,10},{9,11},{10,... | collective-permute-start | bytes 589832 | tf_op jit(solution)/shard_map/ppermute | solution.py:60
  141.0 19.4 %collective-permute-start.21 = (f32[96,768]{1,0:T(8,128)S(1)}, f32[96,768]{1,0:T(8,128)S(1)}, u32[]{:S(2)}, u32[]{:S(2)}) collective-permute-start(f32[96,768]{1,0:T(8,128)S(1)} %collective-permute-done.20), channel_id=1, source_target_pairs={{0,8},{4,12},{8,0},{12,4},{16,24},{20,28},{24,16},{28,20},{1,9},{5... | collective-permute-start | bytes 884744 | tf_op jit(solution)/shard_map/ppermute | solution.py:60
  158.9 10.5 %collective-permute-start.37 = (f32[96,768]{1,0:T(8,128)S(1)}, f32[96,768]{1,0:T(8,128)S(1)}, u32[]{:S(2)}, u32[]{:S(2)}) collective-permute-start(f32[96,768]{1,0:T(8,128)S(1)} %collective-permute-done.36), channel_id=1, source_target_pairs={{0,8},{4,12},{8,0},{12,4},{16,24},{20,28},{24,16},{28,20},{1,9},{5... | collective-permute-start | bytes 884744 | tf_op jit(solution)/shard_map/ppermute | solution.py:60
  160.4 31.2 %collective-permute-start.14 = (f32[64,768]{1,0:T(8,128)S(1)}, f32[64,768]{1,0:T(8,128)S(1)}, u32[]{:S(2)}, u32[]{:S(2)}) collective-permute-start(f32[64,768]{1,0:T(8,128)S(1)} %dynamic-slice_add_fusion.22), channel_id=1, source_target_pairs={{0,2},{1,3},{2,0},{3,1},{4,6},{5,7},{6,4},{7,5},{8,10},{9,11},{10,... | collective-permute-start | bytes 589832 | tf_op jit(solution)/shard_map/ppermute | solution.py:60
  162.6 30.6 %collective-permute-start.10 = (f32[64,768]{1,0:T(8,128)S(1)}, f32[64,768]{1,0:T(8,128)S(1)}, u32[]{:S(2)}, u32[]{:S(2)}) collective-permute-start(f32[64,768]{1,0:T(8,128)S(1)} %dynamic-slice_add_fusion.23), channel_id=1, source_target_pairs={{0,2},{1,3},{2,0},{3,1},{4,6},{5,7},{6,4},{7,5},{8,10},{9,11},{10,... | collective-permute-start | bytes 589832 | tf_op jit(solution)/shard_map/ppermute | solution.py:60
  166.3 27.1 %collective-permute-start.6 = (f32[64,768]{1,0:T(8,128)S(1)}, f32[64,768]{1,0:T(8,128)S(1)}, u32[]{:S(2)}, u32[]{:S(2)}) collective-permute-start(f32[64,768]{1,0:T(8,128)S(1)} %dynamic-slice_add_fusion.24), channel_id=1, source_target_pairs={{0,2},{1,3},{2,0},{3,1},{4,6},{5,7},{6,4},{7,5},{8,10},{9,11},{10,... | collective-permute-start | bytes 589832 | tf_op jit(solution)/shard_map/ppermute | solution.py:60
  166.7 23.3 %collective-permute-start.2 = (f32[64,768]{1,0:T(8,128)S(1)}, f32[64,768]{1,0:T(8,128)S(1)}, u32[]{:S(2)}, u32[]{:S(2)}) collective-permute-start(f32[64,768]{1,0:T(8,128)S(1)} %dynamic-slice_add_fusion.25), channel_id=1, source_target_pairs={{0,2},{1,3},{2,0},{3,1},{4,6},{5,7},{6,4},{7,5},{8,10},{9,11},{10,... | collective-permute-start | bytes 589832 | tf_op jit(solution)/shard_map/ppermute | solution.py:60
  169.4 63.8 %collective-permute-start.18 = (f32[192,768]{1,0:T(8,128)S(1)}, f32[192,768]{1,0:T(8,128)S(1)}, u32[]{:S(2)}, u32[]{:S(2)}) collective-permute-start(f32[192,768]{1,0:T(8,128)S(1)} %pad_maximum_fusion.12), channel_id=1, source_target_pairs={{0,16},{4,20},{8,24},{12,28},{16,0},{20,4},{24,8},{28,12},{1,17},{... | collective-permute-start | bytes 1769480 | tf_op jit(solution)/shard_map/ppermute | solution.py:60
  190.0 50.1 %collective-permute-start.22 = (f32[192,768]{1,0:T(8,128)S(1)}, f32[192,768]{1,0:T(8,128)S(1)}, u32[]{:S(2)}, u32[]{:S(2)}) collective-permute-start(f32[192,768]{1,0:T(8,128)S(1)} %pad_maximum_fusion.13), channel_id=1, source_target_pairs={{0,16},{4,20},{8,24},{12,28},{16,0},{20,4},{24,8},{28,12},{1,17},{... | collective-permute-start | bytes 1769480 | tf_op jit(solution)/shard_map/ppermute | solution.py:60
  191.6 52.0 %collective-permute-start.26 = (f32[192,768]{1,0:T(8,128)S(1)}, f32[192,768]{1,0:T(8,128)S(1)}, u32[]{:S(2)}, u32[]{:S(2)}) collective-permute-start(f32[192,768]{1,0:T(8,128)S(1)} %pad_maximum_fusion.14), channel_id=1, source_target_pairs={{0,8},{4,12},{8,0},{12,4},{16,24},{20,28},{24,16},{28,20},{1,9},{5... | collective-permute-start | bytes 1769480 | tf_op jit(solution)/shard_map/ppermute | solution.py:60
  193.4 55.6 %collective-permute-start.30 = (f32[192,768]{1,0:T(8,128)S(1)}, f32[192,768]{1,0:T(8,128)S(1)}, u32[]{:S(2)}, u32[]{:S(2)}) collective-permute-start(f32[192,768]{1,0:T(8,128)S(1)} %pad_maximum_fusion.15), channel_id=1, source_target_pairs={{0,8},{4,12},{8,0},{12,4},{16,24},{20,28},{24,16},{28,20},{1,9},{5... | collective-permute-start | bytes 1769480 | tf_op jit(solution)/shard_map/ppermute | solution.py:60
  229.1 21.2 %collective-permute-start.34 = (f32[192,768]{1,0:T(8,128)S(1)}, f32[192,768]{1,0:T(8,128)S(1)}, u32[]{:S(2)}, u32[]{:S(2)}) collective-permute-start(f32[192,768]{1,0:T(8,128)S(1)} %pad_maximum_fusion.16), channel_id=1, source_target_pairs={{0,16},{4,20},{8,24},{12,28},{16,0},{20,4},{24,8},{28,12},{1,17},{... | collective-permute-start | bytes 1769480 | tf_op jit(solution)/shard_map/ppermute | solution.py:60
  233.2 21.6 %collective-permute-start.38 = (f32[192,768]{1,0:T(8,128)S(1)}, f32[192,768]{1,0:T(8,128)S(1)}, u32[]{:S(2)}, u32[]{:S(2)}) collective-permute-start(f32[192,768]{1,0:T(8,128)S(1)} %pad_maximum_fusion.17), channel_id=1, source_target_pairs={{0,16},{4,20},{8,24},{12,28},{16,0},{20,4},{24,8},{28,12},{1,17},{... | collective-permute-start | bytes 1769480 | tf_op jit(solution)/shard_map/ppermute | solution.py:60
  240.1 19.6 %collective-permute-start.19 = (f32[384,768]{1,0:T(8,128)S(1)}, f32[384,768]{1,0:T(8,128)S(1)}, u32[]{:S(2)}, u32[]{:S(2)}) collective-permute-start(f32[384,768]{1,0:T(8,128)S(1)} %pad_maximum_fusion.2), channel_id=1, source_target_pairs={{0,4},{4,0},{8,12},{12,8},{16,20},{20,16},{24,28},{28,24},{1,5},{5... | collective-permute-start | bytes 3538952 | tf_op jit(solution)/shard_map/ppermute | solution.py:60
  243.6 25.0 %collective-permute-start.23 = (f32[384,768]{1,0:T(8,128)S(1)}, f32[384,768]{1,0:T(8,128)}, u32[]{:S(2)}, u32[]{:S(2)}) collective-permute-start(f32[384,768]{1,0:T(8,128)S(1)} %pad_maximum_fusion.3), channel_id=1, source_target_pairs={{0,4},{4,0},{8,12},{12,8},{16,20},{20,16},{24,28},{28,24},{1,5},{5... | collective-permute-start | bytes 3538952 | tf_op jit(solution)/shard_map/ppermute | solution.py:60
  248.9 15.3 %collective-permute-start.27 = (f32[384,768]{1,0:T(8,128)S(1)}, f32[384,768]{1,0:T(8,128)S(1)}, u32[]{:S(2)}, u32[]{:S(2)}) collective-permute-start(f32[384,768]{1,0:T(8,128)S(1)} %pad_maximum_fusion.4), channel_id=1, source_target_pairs={{0,4},{4,0},{8,12},{12,8},{16,20},{20,16},{24,28},{28,24},{1,5},{5... | collective-permute-start | bytes 3538952 | tf_op jit(solution)/shard_map/ppermute | solution.py:60
  250.2 32.9 %collective-permute-start.31 = (f32[384,768]{1,0:T(8,128)}, f32[384,768]{1,0:T(8,128)}, u32[]{:S(2)}, u32[]{:S(2)}) collective-permute-start(f32[384,768]{1,0:T(8,128)} %pad_maximum_fusion.5), channel_id=1, source_target_pairs={{0,4},{4,0},{8,12},{12,8},{16,20},{20,16},{24,28},{28,24},{1,5},{5... | collective-permute-start | bytes 3538952 | tf_op jit(solution)/shard_map/ppermute | solution.py:60
  254.9 23.0 %collective-permute-start.35 = (f32[384,768]{1,0:T(8,128)}, f32[384,768]{1,0:T(8,128)}, u32[]{:S(2)}, u32[]{:S(2)}) collective-permute-start(f32[384,768]{1,0:T(8,128)} %pad_maximum_fusion.6), channel_id=1, source_target_pairs={{0,4},{4,0},{8,12},{12,8},{16,20},{20,16},{24,28},{28,24},{1,5},{5... | collective-permute-start | bytes 3538952 | tf_op jit(solution)/shard_map/ppermute | solution.py:60
  259.7 32.7 %collective-permute-start.39 = (f32[384,768]{1,0:T(8,128)}, f32[384,768]{1,0:T(8,128)}, u32[]{:S(2)}, u32[]{:S(2)}) collective-permute-start(f32[384,768]{1,0:T(8,128)} %pad_maximum_fusion.7), channel_id=1, source_target_pairs={{0,4},{4,0},{8,12},{12,8},{16,20},{20,16},{24,28},{28,24},{1,5},{5... | collective-permute-start | bytes 3538952 | tf_op jit(solution)/shard_map/ppermute | solution.py:60
  336.1 21.4 %collective-permute-start.52 = (f32[128,768]{1,0:T(8,128)}, f32[128,768]{1,0:T(8,128)}, u32[]{:S(2)}, u32[]{:S(2)}) collective-permute-start(f32[128,768]{1,0:T(8,128)} %constant_dynamic-slice_fusion.13), channel_id=1, source_target_pairs={{0,1},{1,0},{2,3},{3,2},{4,5},{5,4},{6,7},{7,6},{8,9},{9,8},{10,11... | collective-permute-start | bytes 1179656 | tf_op jit(solution)/shard_map/ppermute | solution.py:60
  337.2 23.2 %collective-permute-start.48 = (f32[128,768]{1,0:T(8,128)}, f32[128,768]{1,0:T(8,128)}, u32[]{:S(2)}, u32[]{:S(2)}) collective-permute-start(f32[128,768]{1,0:T(8,128)} %constant_dynamic-slice_fusion.15), channel_id=1, source_target_pairs={{0,1},{1,0},{2,3},{3,2},{4,5},{5,4},{6,7},{7,6},{8,9},{9,8},{10,11... | collective-permute-start | bytes 1179656 | tf_op jit(solution)/shard_map/ppermute | solution.py:60
  339.7 33.9 %collective-permute-start.44 = (f32[128,768]{1,0:T(8,128)}, f32[128,768]{1,0:T(8,128)}, u32[]{:S(2)}, u32[]{:S(2)}) collective-permute-start(f32[128,768]{1,0:T(8,128)} %constant_dynamic-slice_fusion.17), channel_id=1, source_target_pairs={{0,1},{1,0},{2,3},{3,2},{4,5},{5,4},{6,7},{7,6},{8,9},{9,8},{10,11... | collective-permute-start | bytes 1179656 | tf_op jit(solution)/shard_map/ppermute | solution.py:60
  355.4 26.2 %collective-permute-start.40 = (f32[128,768]{1,0:T(8,128)}, f32[128,768]{1,0:T(8,128)}, u32[]{:S(2)}, u32[]{:S(2)}) collective-permute-start(f32[128,768]{1,0:T(8,128)} %constant_dynamic-slice_fusion.19), channel_id=1, source_target_pairs={{0,1},{1,0},{2,3},{3,2},{4,5},{5,4},{6,7},{7,6},{8,9},{9,8},{10,11... | collective-permute-start | bytes 1179656 | tf_op jit(solution)/shard_map/ppermute | solution.py:60
  358.7 25.0 %collective-permute-start.53 = (f32[64,768]{1,0:T(8,128)S(1)}, f32[64,768]{1,0:T(8,128)S(1)}, u32[]{:S(2)}, u32[]{:S(2)}) collective-permute-start(f32[64,768]{1,0:T(8,128)S(1)} %constant_dynamic-slice_fusion.12), channel_id=1, source_target_pairs={{0,2},{1,3},{2,0},{3,1},{4,6},{5,7},{6,4},{7,5},{8,10},{9,11},{10,... | collective-permute-start | bytes 589832 | tf_op jit(solution)/shard_map/ppermute | solution.py:60
  361.6 24.2 %collective-permute-start.49 = (f32[64,768]{1,0:T(8,128)S(1)}, f32[64,768]{1,0:T(8,128)S(1)}, u32[]{:S(2)}, u32[]{:S(2)}) collective-permute-start(f32[64,768]{1,0:T(8,128)S(1)} %constant_dynamic-slice_fusion.14), channel_id=1, source_target_pairs={{0,2},{1,3},{2,0},{3,1},{4,6},{5,7},{6,4},{7,5},{8,10},{9,11},{10,... | collective-permute-start | bytes 589832 | tf_op jit(solution)/shard_map/ppermute | solution.py:60
  374.7 29.0 %collective-permute-start.45 = (f32[64,768]{1,0:T(8,128)S(1)}, f32[64,768]{1,0:T(8,128)S(1)}, u32[]{:S(2)}, u32[]{:S(2)}) collective-permute-start(f32[64,768]{1,0:T(8,128)S(1)} %constant_dynamic-slice_fusion.16), channel_id=1, source_target_pairs={{0,2},{1,3},{2,0},{3,1},{4,6},{5,7},{6,4},{7,5},{8,10},{9,11},{10,... | collective-permute-start | bytes 589832 | tf_op jit(solution)/shard_map/ppermute | solution.py:60
  382.6 29.5 %collective-permute-start.41 = (f32[64,768]{1,0:T(8,128)S(1)}, f32[64,768]{1,0:T(8,128)S(1)}, u32[]{:S(2)}, u32[]{:S(2)}) collective-permute-start(f32[64,768]{1,0:T(8,128)S(1)} %constant_dynamic-slice_fusion.18), channel_id=1, source_target_pairs={{0,2},{1,3},{2,0},{3,1},{4,6},{5,7},{6,4},{7,5},{8,10},{9,11},{10,... | collective-permute-start | bytes 589832 | tf_op jit(solution)/shard_map/ppermute | solution.py:60
  383.7 36.8 %collective-permute-start.54 = (f32[64,768]{1,0:T(8,128)S(1)}, f32[64,768]{1,0:T(8,128)S(1)}, u32[]{:S(2)}, u32[]{:S(2)}) collective-permute-start(f32[64,768]{1,0:T(8,128)S(1)} %dynamic-slice_add_fusion.18), channel_id=1, source_target_pairs={{0,2},{1,3},{2,0},{3,1},{4,6},{5,7},{6,4},{7,5},{8,10},{9,11},{10,... | collective-permute-start | bytes 589832 | tf_op jit(solution)/shard_map/ppermute | solution.py:60
  385.7 47.6 %collective-permute-start.50 = (f32[64,768]{1,0:T(8,128)S(1)}, f32[64,768]{1,0:T(8,128)S(1)}, u32[]{:S(2)}, u32[]{:S(2)}) collective-permute-start(f32[64,768]{1,0:T(8,128)S(1)} %dynamic-slice_add_fusion.19), channel_id=1, source_target_pairs={{0,2},{1,3},{2,0},{3,1},{4,6},{5,7},{6,4},{7,5},{8,10},{9,11},{10,... | collective-permute-start | bytes 589832 | tf_op jit(solution)/shard_map/ppermute | solution.py:60
  403.7 31.8 %collective-permute-start.46 = (f32[64,768]{1,0:T(8,128)S(1)}, f32[64,768]{1,0:T(8,128)S(1)}, u32[]{:S(2)}, u32[]{:S(2)}) collective-permute-start(f32[64,768]{1,0:T(8,128)S(1)} %dynamic-slice_add_fusion.20), channel_id=1, source_target_pairs={{0,2},{1,3},{2,0},{3,1},{4,6},{5,7},{6,4},{7,5},{8,10},{9,11},{10,... | collective-permute-start | bytes 589832 | tf_op jit(solution)/shard_map/ppermute | solution.py:60
  412.1 21.1 %collective-permute-start.42 = (f32[64,768]{1,0:T(8,128)S(1)}, f32[64,768]{1,0:T(8,128)S(1)}, u32[]{:S(2)}, u32[]{:S(2)}) collective-permute-start(f32[64,768]{1,0:T(8,128)S(1)} %dynamic-slice_add_fusion.21), channel_id=1, source_target_pairs={{0,2},{1,3},{2,0},{3,1},{4,6},{5,7},{6,4},{7,5},{8,10},{9,11},{10,... | collective-permute-start | bytes 589832 | tf_op jit(solution)/shard_map/ppermute | solution.py:60
  420.6 46.4 %collective-permute-start.55 = (f32[128,768]{1,0:T(8,128)S(1)}, f32[128,768]{1,0:T(8,128)S(1)}, u32[]{:S(2)}, u32[]{:S(2)}) collective-permute-start(f32[128,768]{1,0:T(8,128)S(1)} %pad_maximum_fusion.26), channel_id=1, source_target_pairs={{0,1},{1,0},{2,3},{3,2},{4,5},{5,4},{6,7},{7,6},{8,9},{9,8},{10,11... | collective-permute-start | bytes 1179656 | tf_op jit(solution)/shard_map/ppermute | solution.py:60
  433.2 16.8 %collective-permute-start.43 = (f32[128,768]{1,0:T(8,128)S(1)}, f32[128,768]{1,0:T(8,128)S(1)}, u32[]{:S(2)}, u32[]{:S(2)}) collective-permute-start(f32[128,768]{1,0:T(8,128)S(1)} %pad_maximum_fusion.23), channel_id=1, source_target_pairs={{0,1},{1,0},{2,3},{3,2},{4,5},{5,4},{6,7},{7,6},{8,9},{9,8},{10,11... | collective-permute-start | bytes 1179656 | tf_op jit(solution)/shard_map/ppermute | solution.py:60
  433.4 33.5 %collective-permute-start.51 = (f32[128,768]{1,0:T(8,128)S(1)}, f32[128,768]{1,0:T(8,128)S(1)}, u32[]{:S(2)}, u32[]{:S(2)}) collective-permute-start(f32[128,768]{1,0:T(8,128)S(1)} %pad_maximum_fusion.25), channel_id=1, source_target_pairs={{0,1},{1,0},{2,3},{3,2},{4,5},{5,4},{6,7},{7,6},{8,9},{9,8},{10,11... | collective-permute-start | bytes 1179656 | tf_op jit(solution)/shard_map/ppermute | solution.py:60
  435.5 31.2 %collective-permute-start.47 = (f32[128,768]{1,0:T(8,128)S(1)}, f32[128,768]{1,0:T(8,128)S(1)}, u32[]{:S(2)}, u32[]{:S(2)}) collective-permute-start(f32[128,768]{1,0:T(8,128)S(1)} %pad_maximum_fusion.24), channel_id=1, source_target_pairs={{0,1},{1,0},{2,3},{3,2},{4,5},{5,4},{6,7},{7,6},{8,9},{9,8},{10,11... | collective-permute-start | bytes 1179656 | tf_op jit(solution)/shard_map/ppermute | solution.py:60
  481.5 17.7 %collective-permute-start.56 = (f32[416,384]{1,0:T(8,128)}, f32[416,384]{1,0:T(8,128)}, u32[]{:S(2)}, u32[]{:S(2)}) collective-permute-start(f32[416,384]{1,0:T(8,128)} %constant_dynamic-slice_fusion.11), channel_id=1, source_target_pairs={{0,4},{4,0},{8,12},{12,8},{16,20},{20,16},{24,28},{28,24},{1,5},{5... | collective-permute-start | bytes 1916936 | tf_op jit(solution)/shard_map/ppermute | solution.py:60
  482.4 19.1 %collective-permute-start.62 = (f32[416,384]{1,0:T(8,128)S(1)}, f32[416,384]{1,0:T(8,128)}, u32[]{:S(2)}, u32[]{:S(2)}) collective-permute-start(f32[416,384]{1,0:T(8,128)S(1)} %constant_dynamic-slice_fusion.8), channel_id=1, source_target_pairs={{0,4},{4,0},{8,12},{12,8},{16,20},{20,16},{24,28},{28,24},{1,5},{5... | collective-permute-start | bytes 1916936 | tf_op jit(solution)/shard_map/ppermute | solution.py:60
  498.6 20.9 %collective-permute-start.68 = (f32[800,384]{1,0:T(8,128)S(1)}, f32[800,384]{1,0:T(8,128)S(1)}, u32[]{:S(2)}, u32[]{:S(2)}) collective-permute-start(f32[800,384]{1,0:T(8,128)S(1)} %constant_dynamic-slice_fusion.5), channel_id=1, source_target_pairs={{0,4},{4,0},{8,12},{12,8},{16,20},{20,16},{24,28},{28,24},{1,5},{5... | collective-permute-start | bytes 3686408 | tf_op jit(solution)/shard_map/ppermute | solution.py:60
  498.7 21.0 %collective-permute-start.74 = (f32[800,384]{1,0:T(8,128)S(1)}, f32[800,384]{1,0:T(8,128)S(1)}, u32[]{:S(2)}, u32[]{:S(2)}) collective-permute-start(f32[800,384]{1,0:T(8,128)S(1)} %constant_dynamic-slice_fusion.2), channel_id=1, source_target_pairs={{0,4},{4,0},{8,12},{12,8},{16,20},{20,16},{24,28},{28,24},{1,5},{5... | collective-permute-start | bytes 3686408 | tf_op jit(solution)/shard_map/ppermute | solution.py:60
  519.7 22.1 %collective-permute-start.69 = (f32[400,384]{1,0:T(8,128)S(1)}, f32[400,384]{1,0:T(8,128)S(1)}, u32[]{:S(2)}, u32[]{:S(2)}) collective-permute-start(f32[400,384]{1,0:T(8,128)S(1)} %constant_dynamic-slice_fusion.4), channel_id=1, source_target_pairs={{0,8},{4,12},{8,0},{12,4},{16,24},{20,28},{24,16},{28,20},{1,9},{5... | collective-permute-start | bytes 1843208 | tf_op jit(solution)/shard_map/ppermute | solution.py:60
  520.0 22.6 %collective-permute-start.75 = (f32[400,384]{1,0:T(8,128)S(1)}, f32[400,384]{1,0:T(8,128)S(1)}, u32[]{:S(2)}, u32[]{:S(2)}) collective-permute-start(f32[400,384]{1,0:T(8,128)S(1)} %constant_dynamic-slice_fusion.1), channel_id=1, source_target_pairs={{0,16},{4,20},{8,24},{12,28},{16,0},{20,4},{24,8},{28,12},{1,17},{... | collective-permute-start | bytes 1843208 | tf_op jit(solution)/shard_map/ppermute | solution.py:60
  522.5 19.0 %collective-permute-start.60 = (f32[208,384]{1,0:T(8,128)S(1)}, f32[208,384]{1,0:T(8,128)S(1)}, u32[]{:S(2)}, u32[]{:S(2)}) collective-permute-start(f32[208,384]{1,0:T(8,128)S(1)} %pad_maximum_fusion.27), channel_id=1, source_target_pairs={{0,8},{4,12},{8,0},{12,4},{16,24},{20,28},{24,16},{28,20},{1,9},{5... | collective-permute-start | bytes 958472 | tf_op jit(solution)/shard_map/ppermute | solution.py:60
  524.6 17.1 %collective-permute-start.66 = (f32[208,384]{1,0:T(8,128)S(1)}, f32[208,384]{1,0:T(8,128)S(1)}, u32[]{:S(2)}, u32[]{:S(2)}) collective-permute-start(f32[208,384]{1,0:T(8,128)S(1)} %pad_maximum_fusion.28), channel_id=1, source_target_pairs={{0,16},{4,20},{8,24},{12,28},{16,0},{20,4},{24,8},{28,12},{1,17},{... | collective-permute-start | bytes 958472 | tf_op jit(solution)/shard_map/ppermute | solution.py:60
  541.6 12.4 %collective-permute-start.61 = (f32[416,384]{1,0:T(8,128)S(1)}, f32[416,384]{1,0:T(8,128)S(1)}, u32[]{:S(2)}, u32[]{:S(2)}) collective-permute-start(f32[416,384]{1,0:T(8,128)S(1)} %pad_maximum_fusion.8), channel_id=1, source_target_pairs={{0,4},{4,0},{8,12},{12,8},{16,20},{20,16},{24,28},{28,24},{1,5},{5... | collective-permute-start | bytes 1916936 | tf_op jit(solution)/shard_map/ppermute | solution.py:60
  544.4 18.7 %collective-permute-start.67 = (f32[416,384]{1,0:T(8,128)S(1)}, f32[416,384]{1,0:T(8,128)S(1)}, u32[]{:S(2)}, u32[]{:S(2)}) collective-permute-start(f32[416,384]{1,0:T(8,128)S(1)} %pad_maximum_fusion.9), channel_id=1, source_target_pairs={{0,4},{4,0},{8,12},{12,8},{16,20},{20,16},{24,28},{28,24},{1,5},{5... | collective-permute-start | bytes 1916936 | tf_op jit(solution)/shard_map/ppermute | solution.py:60
  552.5 9.8 %collective-permute-start.77 = (f32[200,384]{1,0:T(8,128)S(1)}, f32[200,384]{1,0:T(8,128)S(1)}, u32[]{:S(2)}, u32[]{:S(2)}) collective-permute-start(f32[200,384]{1,0:T(8,128)S(1)} %dynamic-slice_add_fusion.16), channel_id=1, source_target_pairs={{0,8},{4,12},{8,0},{12,4},{16,24},{20,28},{24,16},{28,20},{1,9},{5... | collective-permute-start | bytes 921608 | tf_op jit(solution)/shard_map/ppermute | solution.py:60
  560.7 14.6 %collective-permute-start.72 = (f32[400,384]{1,0:T(8,128)S(1)}, f32[400,384]{1,0:T(8,128)S(1)}, u32[]{:S(2)}, u32[]{:S(2)}) collective-permute-start(f32[400,384]{1,0:T(8,128)S(1)} %pad_maximum_fusion.10), channel_id=1, source_target_pairs={{0,8},{4,12},{8,0},{12,4},{16,24},{20,28},{24,16},{28,20},{1,9},{5... | collective-permute-start | bytes 1843208 | tf_op jit(solution)/shard_map/ppermute | solution.py:60
  562.4 14.4 %collective-permute-start.78 = (f32[400,384]{1,0:T(8,128)S(1)}, f32[400,384]{1,0:T(8,128)S(1)}, u32[]{:S(2)}, u32[]{:S(2)}) collective-permute-start(f32[400,384]{1,0:T(8,128)S(1)} %pad_maximum_fusion.11), channel_id=1, source_target_pairs={{0,16},{4,20},{8,24},{12,28},{16,0},{20,4},{24,8},{28,12},{1,17},{... | collective-permute-start | bytes 1843208 | tf_op jit(solution)/shard_map/ppermute | solution.py:60
  576.6 14.3 %collective-permute-start.73 = (f32[800,384]{1,0:T(8,128)}, f32[800,384]{1,0:T(8,128)}, u32[]{:S(2)}, u32[]{:S(2)}) collective-permute-start(f32[800,384]{1,0:T(8,128)} %pad_maximum_fusion), channel_id=1, source_target_pairs={{0,4},{4,0},{8,12},{12,8},{16,20},{20,16},{24,28},{28,24},{1,5},{5... | collective-permute-start | bytes 3686408 | tf_op jit(solution)/shard_map/ppermute | solution.py:60
  578.0 14.5 %collective-permute-start.79 = (f32[800,384]{1,0:T(8,128)}, f32[800,384]{1,0:T(8,128)}, u32[]{:S(2)}, u32[]{:S(2)}) collective-permute-start(f32[800,384]{1,0:T(8,128)} %pad_maximum_fusion.1), channel_id=1, source_target_pairs={{0,4},{4,0},{8,12},{12,8},{16,20},{20,16},{24,28},{28,24},{1,5},{5... | collective-permute-start | bytes 3686408 | tf_op jit(solution)/shard_map/ppermute | solution.py:60
  (136 other events, 1621.8 us)

commit v2 on v0

--- a/solution.py
+++ b/solution.py
@@ -1,6 +1,8 @@
 import jax
 import jax.numpy as jnp
 from jax import lax
+from jax.experimental import pallas as pl
+from jax.experimental.pallas import tpu as pltpu
 from jax.sharding import PartitionSpec as P
 
 HD = 64
@@ -54,6 +56,301 @@
         "hqd,hkd->hqk", query_block, key_heads, preferred_element_type=jnp.float32
     ) * HD ** (-0.5)
     return jnp.where(allowed[None], scores, NEGATIVE)
+
+
+def bits_of(size):
+    return [1 << i for i in range(size.bit_length() - 1)]
+
+
+def bit_of(axis, bit):
+    return (lax.axis_index(axis) // bit) % 2
+
+
+def partner(axis, bit):
+    me = lax.axis_index(axis)
+    for one in bits_of(lax.axis_size(axis)):
+        if bit & one:
+            me = me + one - 2 * one * bit_of(axis, one)
+    return {axis: me}
+
+
+def greet(partners):
+    barrier = pltpu.get_barrier_semaphore()
+    for device in partners:
+        pl.semaphore_signal(
+            barrier, inc=1, device_id=device, device_id_type=pl.DeviceIdType.MESH
+        )
+    pl.semaphore_wait(barrier, len(partners))
+
+
+class Copies:
+    def __init__(self, send_sems, recv_sems):
+        self.sems, self.used = (send_sems, recv_sems), 0
+
+    def start(self, source, target, device):
+        at, self.used = self.used, self.used + 1
+        copy = pltpu.make_async_remote_copy(
+            src_ref=source,
+            dst_ref=target,
+            send_sem=self.sems[0].at[at],
+            recv_sem=self.sems[1].at[at],
+            device_id=device,
+            device_id_type=pl.DeviceIdType.MESH,
+        )
+        copy.start()
+        return copy
+
+
+def sum_stream(copies, source, acc, recv, first, rows, steps):
+    base, at, held = first, 0, []
+    origin, start = source, first
+    for number, (axis, bit) in enumerate(steps):
+        half = rows >> (number + 1)
+        mine = bit_of(axis, bit)
+        keep = pl.multiple_of(start + mine * half, 8)
+        give = pl.multiple_of(start + (1 - mine) * half, 8)
+        landing = recv.at[pl.ds(at, half)]
+        copy = copies.start(origin.at[pl.ds(give, half)], landing, partner(axis, bit))
+        yield
+        copy.wait()
+        recv[pl.ds(at, half), :] = recv[pl.ds(at, half), :] + origin[pl.ds(keep, half), :]
+        base = pl.multiple_of(base + mine * half, 8)
+        origin, start, at = recv, at, at + half
+        held.append((base, half))
+    acc[pl.ds(base, half), :] = recv[pl.ds(start, half), :]
+    for (axis, bit), (keep, half) in zip(reversed(steps), reversed(held)):
+        window = acc.at[pl.ds(keep, half)]
+        copy = copies.start(window, window, partner(axis, bit))
+        yield
+        copy.wait()
+
+
+def run_streams(streams):
+    streams = list(streams)
+    while streams:
+        streams = [stream for stream in streams if next(stream, streams) is not streams]
+
+
+PARTS = 4
+MESH_PARAMS = dict(has_side_effects=True, vmem_limit_bytes=56 * 2**20)
+
+
+def tensor_streams(copies, source, acc, recv, bits):
+    rows = acc.shape[0] // PARTS
+    return [
+        sum_stream(
+            copies,
+            source,
+            acc,
+            recv.at[pl.ds(part * rows, rows)],
+            part * rows,
+            rows,
+            [("tensor", bit) for bit in bits],
+        )
+        for part in range(PARTS)
+    ]
+
+
+def front_kernel(
+    dp_bits, t_bits, part_ref, up_ref, down_ref, bias_ref, sum_ref, ups_ref, downs_ref,
+    biases_ref, recv, wide, send_sems, recv_sems,
+):
+    greet(
+        [partner("tensor", b) for b in range(1, biases_ref.shape[0] + 1)]
+        + [partner("dp", b) for b in dp_bits]
+    )
+    copies = Copies(send_sems, recv_sems)
+    others = biases_ref.shape[0]
+    near, far = dp_bits[:1], dp_bits[1:]
+    count = up_ref.shape[0]
+
+    def gather(kind, other, piece, done):
+        lead = 1 << (other.bit_length() - 1)
+        rest = other - lead
+        place = wide.at[kind, other - 1]
+        if rest == 0:
+            origin, link = piece, lead
+        else:
+            while lead not in done:
+                yield
+            origin, link = wide.at[kind, lead - 1, pl.ds(0, count)], rest
+        copy = copies.start(origin, place.at[pl.ds(0, count)], partner("tensor", link))
+        yield
+        copy.wait()
+        done.add(other)
+        rows = count
+        order = (far if other % 2 else far[::-1]) + near
+        for bit in order:
+            copy = copies.start(
+                place.at[pl.ds(0, rows)], place.at[pl.ds(rows, rows)], partner("dp", bit)
+            )
+            yield
+            copy.wait()
+            rows = 2 * rows
+        out = (ups_ref, downs_ref)[kind]
+
+        def narrow(step, carry):
+            window = pl.ds(pl.multiple_of(step * 32, 32), 32)
+            out[other - 1, window, :] = wide[kind, other - 1, window, :].astype(jnp.bfloat16)
+            return carry
+
+        lax.fori_loop(0, rows // 32, narrow, 0)
+
+    def bias_stream(other):
+        copy = copies.start(bias_ref, biases_ref.at[other - 1], partner("tensor", other))
+        yield
+        copy.wait()
+
+    done = (set(), set())
+    run_streams(
+        [gather(0, o, up_ref, done[0]) for o in range(1, others + 1)]
+        + [gather(1, o, down_ref, done[1]) for o in range(1, others + 1)]
+        + tensor_streams(copies, part_ref, sum_ref, recv, t_bits)
+        + [bias_stream(o) for o in range(1, others + 1)]
+    )
+
+
+def unit_order(other, size):
+    bits = bits_of(size)
+    near, far = bits[:1], bits[1:]
+    order = jnp.arange(1) ^ (lax.axis_index("dp") % size)
+    for bit in (far if other % 2 else far[::-1]) + near:
+        order = jnp.concatenate([order, order ^ bit])
+    return order
+
+
+def front(partial, w_up, w_down, bias_up):
+    others = lax.axis_size("tensor") - 1
+    units, width = w_down.shape
+    size = lax.axis_size("dp")
+    while units % (8 * size):
+        size = size // 2
+    place, count = lax.axis_index("dp") % size, units // size
+    up_piece = lax.dynamic_slice_in_dim(w_up, place * count, count, 1).T.astype(jnp.float32)
+    down_piece = lax.dynamic_slice_in_dim(w_down, place * count, count, 0).astype(jnp.float32)
+    bias_block = jnp.broadcast_to(bias_up[None], (8, units))
+    dp_bits, t_bits = bits_of(size), bits_of(others + 1)
+    total_copies = 2 * others * (1 + len(dp_bits)) + others + PARTS * 2 * len(t_bits)
+    vmem = pl.BlockSpec(memory_space=pltpu.VMEM)
+
+    def body(*refs):
+        front_kernel(dp_bits, t_bits, *refs)
+
+    total, ups, downs, biases = pl.pallas_call(
+        body,
+        out_shape=[
+            jax.ShapeDtypeStruct(partial.shape, jnp.float32),
+            jax.ShapeDtypeStruct((others, units, width), jnp.bfloat16),
+            jax.ShapeDtypeStruct((others, units, width), jnp.bfloat16),
+            jax.ShapeDtypeStruct((others, 8, units), jnp.float32),
+        ],
+        in_specs=[vmem] * 4,
+        out_specs=[vmem] * 4,
+        scratch_shapes=[
+            pltpu.VMEM(partial.shape, jnp.float32),
+            pltpu.VMEM((2, others, units, width), jnp.float32),
+            pltpu.SemaphoreType.DMA((total_copies,)),
+            pltpu.SemaphoreType.DMA((total_copies,)),
+        ],
+        compiler_params=pltpu.CompilerParams(collective_id=0, **MESH_PARAMS),
+    )(partial, up_piece, down_piece, bias_block)
+    found = []
+    for other in range(1, others + 1):
+        bias = biases[other - 1, 0].reshape(size, count)[unit_order(other, size)].reshape(-1)
+        found.append((ups[other - 1], downs[other - 1], bias))
+    return total, found
+
+
+def back_kernel(
+    dp_bits, t_bits, part_ref, *refs,
+):
+    count = (len(refs) - 9) // 2
+    given, sum_ref, wanted = refs[:count], refs[count], refs[count + 1 : 2 * count + 1]
+    acc, loaded, recv, dp_recv, small_recv, send_sems, recv_sems, local_sems = refs[2 * count + 1 :]
+    loads, at = [], 0
+    for number, ref in enumerate(given):
+        rows = ref.shape[0]
+        loads.append(
+            pltpu.make_async_copy(ref, loaded.at[pl.ds(at, rows)], local_sems.at[number])
+        )
+        at = at + rows
+    for load in loads:
+        load.start()
+    greet([partner("tensor", b) for b in t_bits] + [partner("dp", b) for b in dp_bits])
+    copies = Copies(send_sems, recv_sems)
+    near, far = dp_bits[:1], dp_bits[1:]
+    half = acc.shape[0] // 2
+
+    def dp_stream(part):
+        order = near + (far if part == 0 else far[::-1])
+        return sum_stream(
+            copies,
+            loaded,
+            acc,
+            dp_recv.at[pl.ds(part * half, half)],
+            part * half,
+            half,
+            [("dp", bit) for bit in order],
+        )
+
+    def last_stream():
+        yield from dp_stream(1)
+        rows = pl.ds(acc.shape[0] - given[-1].shape[0], 8)
+        for number, bit in enumerate(t_bits):
+            copy = copies.start(acc.at[rows], small_recv.at[number], partner("tensor", bit))
+            yield
+            copy.wait()
+            acc[rows, :] = acc[rows, :] + small_recv[number]
+
+    streams = tensor_streams(copies, part_ref, sum_ref, recv, t_bits)
+    for stream in streams:
+        next(stream)
+    for load in loads:
+        load.wait()
+    run_streams([dp_stream(0), last_stream()] + streams)
+    stores, at = [], 0
+    for number, ref in enumerate(wanted):
+        rows = ref.shape[0]
+        stores.append(
+            pltpu.make_async_copy(acc.at[pl.ds(at, rows)], ref, local_sems.at[count + number])
+        )
+        at = at + rows
+    for store in stores:
+        store.start()
+    for store in stores:
+        store.wait()
+
+
+def back(partial, blocks):
+    unit = 16 * lax.axis_size("dp")
+    short = -sum(block.shape[0] for block in blocks) % unit
+    blocks = [*blocks[:-1], jnp.pad(blocks[-1], ((0, short), (0, 0)))]
+    dp_bits, t_bits = bits_of(lax.axis_size("dp")), bits_of(lax.axis_size("tensor"))
+    rows = sum(block.shape[0] for block in blocks)
+    width = partial.shape[1]
+    total_copies = PARTS * 2 * len(t_bits) + 4 * len(dp_bits) + len(t_bits)
+    vmem, anywhere = pl.BlockSpec(memory_space=pltpu.VMEM), pl.BlockSpec(memory_space=pl.ANY)
+
+    def body(*refs):
+        back_kernel(dp_bits, t_bits, *refs)
+
+    return pl.pallas_call(
+        body,
+        out_shape=[jax.ShapeDtypeStruct(v.shape, jnp.float32) for v in (partial, *blocks)],
+        in_specs=[vmem] + [anywhere] * len(blocks),
+        out_specs=[vmem] + [anywhere] * len(blocks),
+        scratch_shapes=[
+            pltpu.VMEM((rows, width), jnp.float32),
+            pltpu.VMEM((rows, width), jnp.float32),
+            pltpu.VMEM(partial.shape, jnp.float32),
+            pltpu.VMEM((rows, width), jnp.float32),
+            pltpu.VMEM((len(t_bits), 8, width), jnp.float32),
+            pltpu.SemaphoreType.DMA((total_copies,)),
+            pltpu.SemaphoreType.DMA((total_copies,)),
+            pltpu.SemaphoreType.DMA((2 * len(blocks),)),
+        ],
+        compiler_params=pltpu.CompilerParams(collective_id=1, **MESH_PARAMS),
+    )(partial, *blocks)
 
 
 def per_device(
@@ -109,28 +406,31 @@
         logsum_blocks.append(row_top + jnp.log(row_total))
     attended_seqs = heads_last(jnp.concatenate(mixed_blocks, axis=1))
     attended_low = attended_seqs.astype(jnp.bfloat16)
-    attention_total = lax.psum(matmul(attended_low, w_out), "tensor")
+    attention_total, others = front(matmul(attended_low, w_out), w_up, w_down, bias_up)
     hidden_one = inputs + attention_total + bias_out
     normed_two, norm_two_back = jax.vjp(layer_norm, hidden_one, ln2_gain, ln2_shift)
     normed_two_low = normed_two.astype(jnp.bfloat16)
+    grad_out = cotangent.astype(jnp.float32)
     pre_act = matmul(normed_two_low, w_up) + bias_up
     activated, act_back = jax.vjp(smooth_unit, pre_act)
     activated_low = activated.astype(jnp.bfloat16)
-    feed_total = lax.psum(matmul(activated_low, w_down), "tensor")
-    output = (hidden_one + feed_total + bias_down).astype(jnp.bfloat16)
-    grad_out = cotangent.astype(jnp.float32)
+    feed_total = matmul(activated_low, w_down)
     grad_w_down = inner_rows(activated_low, cotangent)
     grad_bias_down = jnp.sum(grad_out, axis=0)
     (grad_pre,) = act_back(inner_cols(cotangent, w_down))
     grad_pre_low = grad_pre.astype(jnp.bfloat16)
     grad_w_up = inner_rows(normed_two_low, grad_pre_low)
     grad_bias_up = jnp.sum(grad_pre_low.astype(jnp.float32), axis=0)
-    grad_normed_two = lax.psum(inner_cols(grad_pre_low, w_up), "tensor")
+    grad_normed_two = inner_cols(grad_pre_low, w_up)
+    for up_part, down_part, bias_part in others:
+        pre_act = inner_cols(normed_two_low, up_part) + bias_part
+        activated, act_back = jax.vjp(smooth_unit, pre_act)
+        feed_total = feed_total + matmul(activated.astype(jnp.bfloat16), down_part)
+        (grad_pre,) = act_back(inner_cols(cotangent, down_part))
+        grad_normed_two = grad_normed_two + matmul(grad_pre.astype(jnp.bfloat16), up_part)
+    output = (hidden_one + feed_total + bias_down).astype(jnp.bfloat16)
     grad_hidden_part, grad_ln2_gain, grad_ln2_shift = norm_two_back(grad_normed_two)
     grad_hidden = grad_out + grad_hidden_part
-    grad_ln2_gain, grad_ln2_shift, grad_w_up, grad_bias_up, grad_w_down, grad_bias_down = lax.psum(
-        (grad_ln2_gain, grad_ln2_shift, grad_w_up, grad_bias_up, grad_w_down, grad_bias_down), "dp"
-    )
     grad_hidden_low = grad_hidden.astype(jnp.bfloat16)
     grad_w_out = inner_rows(attended_low, grad_hidden_low)
     grad_bias_out = jnp.sum(grad_hidden, axis=0)
@@ -174,43 +474,63 @@
     grad_query_low = grad_query_seqs.astype(jnp.bfloat16)
     grad_key_low = grad_key_seqs.astype(jnp.bfloat16)
     grad_value_low = grad_value_seqs.astype(jnp.bfloat16)
-    grad_w_query = inner_rows(normed_low, grad_query_low)
-    grad_bias_query = jnp.sum(grad_query_low.astype(jnp.float32), axis=0)
-    grad_w_key = inner_rows(normed_low, grad_key_low)
-    grad_w_value = inner_rows(normed_low, grad_value_low)
-    grad_bias_value = jnp.sum(grad_value_low.astype(jnp.float32), axis=0)
     grad_normed_part = (
         inner_cols(grad_query_low, w_query)
         + inner_cols(grad_key_low, w_key)
         + inner_cols(grad_value_low, w_value)
     )
-    grad_normed_one = lax.psum(grad_normed_part, "tensor")
-    grad_input_part, grad_ln1_gain, grad_ln1_shift = norm_one_back(grad_normed_one)
-    grad_input = grad_hidden + grad_input_part
+    grad_bias_query = jnp.sum(grad_query_low.astype(jnp.float32), axis=0)
+    grad_bias_value = jnp.sum(grad_value_low.astype(jnp.float32), axis=0)
+    _, grad_ln1_gain, grad_ln1_shift = norm_one_back(grad_normed_part)
+    held, width = w_query.shape[1], w_query.shape[0]
+    head_bias = jnp.concatenate(
+        [grad_bias_query, grad_bias_value, jnp.zeros((width - 2 * held,), jnp.float32)]
+    )
+    small = jnp.concatenate(
+        [
+            jnp.stack([grad_ln1_gain, grad_ln1_shift]),
+            jnp.zeros((6, width), jnp.float32),
+            jnp.stack(
+                [
+                    grad_bias_out,
+                    head_bias,
+                    grad_ln2_gain,
+                    grad_ln2_shift,
+                    grad_bias_up,
+                    grad_bias_down,
+                ]
+            ),
+            jnp.zeros((2, width), jnp.float32),
+        ]
+    )
     (
-        grad_ln1_gain,
-        grad_ln1_shift,
+        grad_normed_one,
+        grad_w_up,
+        grad_w_down,
         grad_w_query,
-        grad_bias_query,
         grad_w_key,
         grad_w_value,
-        grad_bias_value,
         grad_w_out,
-        grad_bias_out,
-    ) = lax.psum(
-        (
-            grad_ln1_gain,
-            grad_ln1_shift,
-            grad_w_query,
-            grad_bias_query,
-            grad_w_key,
-            grad_w_value,
-            grad_bias_value,
+        small,
+    ) = back(
+        grad_normed_part,
+        [
+            grad_w_up,
+            grad_w_down,
+            inner_rows(grad_query_low, normed_low),
+            inner_rows(grad_key_low, normed_low),
+            inner_rows(grad_value_low, normed_low),
             grad_w_out,
-            grad_bias_out,
-        ),
-        "dp",
-    )
+            small,
+        ],
+    )
+    grad_w_query, grad_w_key, grad_w_value = grad_w_query.T, grad_w_key.T, grad_w_value.T
+    grad_ln1_gain, grad_ln1_shift = small[0], small[1]
+    grad_bias_out = small[8]
+    grad_bias_query, grad_bias_value = small[9, :held], small[9, held : 2 * held]
+    grad_ln2_gain, grad_ln2_shift, grad_bias_up, grad_bias_down = small[10:14]
+    grad_input_part, _, _ = norm_one_back(grad_normed_one)
+    grad_input = grad_hidden + grad_input_part
     return (
         output,
         grad_input,

time: 679 us -> 526 us (0.77)
  waiting for transfers between devices: 523 us -> 0 us
  Pallas kernels: 0 us -> 338 us
  matrix products: 53.6 us -> 120 us
  blocking collectives: 26 us -> 0 us
  between operations: 15.1 us -> 1.94 us
  local copies, waits for them, and re-layouts: 16.8 us -> 24 us
    psum x4 -> x0, waiting for transfers between devices: 523 us -> none  [the longest x1 207 us: per_device(): feed_total = lax.psum(matmul(activated_low, w_down), 'tensor')]
    pallas_call x0 -> x2, Pallas kernels: none -> 338 us  [the longest x1 172 us: front(): pl.pallas_call(body, out_shape=[jax.ShapeDtypeStruct(partial.shape, jnp.f...]
    dot_general x6 -> x12, matrix products: 11.3 us -> 60.3 us  [matmul(): return jnp.dot(left_side, right_side, preferred_element_type=jnp.float32)]
    psum x1 -> x0, blocking collectives: 26 us -> none  [per_device(): lax.psum((grad_ln1_gain, grad_ln1_shift, grad_w_query, grad_bias_query, g...]
    dot_general x6 -> x9, matrix products: 11.8 us -> 28 us  [inner_cols(): lax.dot_general(left_side, right_side, (((1,), (1,)), ((), ())), preferre...]
    unnamed x148 -> x181, local copies, waits for them, and re-layouts: 16.7 us -> 14.6 us
  transfers between devices with their start and end apart: 4 -> 0, of which waited for: 4 -> 0; matrix products, arithmetic and copies ran while one was open for 5% -> 0% of each run, Pallas kernels for 0% -> 0%
where the time goes in v2:
time: 526 us; the launch traced here: 517 us
  Pallas kernels  338 us (64%)
  matrix products  120 us (23%)
  other arithmetic  32.5 us (6%)
  local copies, waits for them, and re-layouts  24 us (5%)
    pallas_call x1, Pallas kernels, front(): pl.pallas_call(body, out_shape=[jax.ShapeDtypeStruct(partial.shape, jnp.f...  172 us
    pallas_call x1, Pallas kernels, back(): pl.pallas_call(body, out_shape=[jax.ShapeDtypeStruct(v.shape, jnp.float32...  166 us
    dot_general x12, matrix products, matmul(): return jnp.dot(left_side, right_side, preferred_element_type=jnp.float32)  60.3 us
    dot_general x9, matrix products, inner_cols(): lax.dot_general(left_side, right_side, (((1,), (1,)), ((), ())), preferre...  28 us
    unnamed x181, local copies, waits for them, and re-layouts  14.6 us
    dot_general x6, matrix products, inner_rows(): lax.dot_general(left_side, right_side, (((0,), (0,)), ((), ())), preferre...  11.8 us

profile of v2, /device:TPU:0, one launch (start us, length us, event | category | flops | bytes accessed | tf_op | source)
XLA Modules:
  0.0 517.3 jit_solution(16824546213965492334)
XLA Ops:
  0.7 1.8 convert_reduce_fusion
  2.6 2.0 fusion.41
  8.0 1.1 fusion.61
  9.2 1.4 fusion.177
  10.6 1.5 fusion.1
  12.1 1.1 copy-done.3
  13.3 1.6 fusion.99
  15.0 1.4 fusion.178
  16.4 1.5 fusion
  17.9 1.1 copy-done.2
  19.1 1.7 fusion.100
  20.8 2.3 fusion.181.refs_0_
  23.1 0.8 constant_dynamic-slice_fusion
  23.9 1.7 copy.42
  25.6 1.6 convert_bitcast_fusion.refs_1_
  27.2 1.6 dynamic-slice_convert_fusion.refs_2_
  29.5 172.3 %shard_map.308 = (f32[1024,768]{1,0:T(8,128)}, bf16[3,768,768]{2,1,0:T(8,128)(2,1)}, bf16[3,768,768]{2,1,0:T(8,128)(2,1)}, f32[3,8,768]{2,1,0:T(8,128)}) custom-call(f32[1024,768]{1,0:T(8,128)} %fusion.181.refs_0_, f32[96,768]{1,0:T(8,128)} %convert_bitcast_fusion.refs_1_, f32[96,768]{1,0:T(8,128)} %dynamic-slice_convert_fusion.refs_2_, ...), custom_call_target="tpu_custom_call" | custom-call | tf_op jit(solution)/shard_map/pallas_call | solution.py:239
  201.8 2.4 fusion.173
  205.9 4.9 fusion.91
  210.8 1.4 slice_reduce_fusion.7
  215.3 6.1 %fusion.68 = f32[1024,768]{1,0:T(8,128)} fusion(f32[1024,768]{1,0:T(8,128)} %fusion.91, f32[768]{0:T(1024)S(1)} %add.268, bf16[3,768,768]{2,1,0:T(8,128)(2,1)} %get-tuple-element.32), kind=kOutput, calls=%fused_computation.117 | convolution fusion | flops 1215823872 | bytes 7474176 | tf_op jit(solution)/shard_map/dot_general | solution.py:26
  221.3 1.4 fusion.182
  222.8 3.8 fusion.168
  226.6 4.4 fusion.97
  231.0 1.3 pad_clamp_fusion.1
  233.1 6.0 %fusion.67 = f32[1024,768]{1,0:T(8,128)} fusion(f32[1024,768]{1,0:T(8,128)} %fusion.97, f32[768]{0:T(1024)S(1)} %add.261, bf16[3,768,768]{2,1,0:T(8,128)(2,1)} %get-tuple-element.32), kind=kOutput, calls=%fused_computation.116 | convolution fusion | flops 1215823872 | bytes 7474176 | tf_op jit(solution)/shard_map/dot_general | solution.py:26
  239.1 4.4 fusion.85
  244.3 9.6 %add_convert_fusion = bf16[1024,768]{1,0:T(8,128)(2,1)} fusion(f32[1024,768]{1,0:T(8,128)} %copy-done.7, f32[1024,768]{1,0:T(8,128)} %fusion.68, f32[1024,768]{1,0:T(8,128)} %fusion.168, f32[1024,768]{1,0:T(8,128)} %fusion.67, f32[768]{0:T(1024)} %param.34, f32[1024,768]{1,0:T(8,128)} %fusion.85, f32[768]{0:T(1024)S(1)} %add.274, ...), kind=kOutput, calls=%fused_computation.99 | convolution fusion | flops 1220542464 | bytes 18488320 | tf_op jit(solution)/shard_map/dot_general | solution.py:26
  254.0 8.6 %fusion.69 = f32[1024,768]{1,0:T(8,128)} fusion(f32[1024,768]{1,0:T(8,128)} %fusion.91, bf16[1024,768]{1,0:T(8,128)(2,1)} %param.35, f32[768]{0:T(1024)} %copy-done.73, bf16[3,768,768]{2,1,0:T(8,128)(2,1)} %get-tuple-element.32, bf16[3,768,768]{2,1,0:T(8,128)(2,1)} %get-tuple-element.30), kind=kOutput, calls=%fused_computation.118 | convolution fusion | flops 2432434176 | bytes 10227712 | tf_op jit(solution)/shard_map/dot_general | solution.py:26
  262.6 6.3 %convert_reduce_fusion.2 = (f32[768]{0:T(1024)}, bf16[1024,768]{1,0:T(8,128)(2,1)S(1)}) fusion(f32[1024,768]{1,0:T(8,128)} %copy-done.79, f32[768]{0:T(1024)S(1)} %copy-done.68, bf16[1024,768]{1,0:T(8,128)(2,1)} %param.35, bf16[768,768]{1,0:T(8,128)(2,1)} %param.33), kind=kOutput, calls=%fused_computation.92 | convolution fusion | flops 1226046720 | bytes 7477248 | tf_op jit(solution)/shard_map/dot_general | solution.py:36
  268.9 1.1 copy-done.81
  270.0 3.1 fusion.183
  273.1 9.0 %fusion.70 = f32[1024,768]{1,0:T(8,128)} fusion(f32[1024,768]{1,0:T(8,128)} %fusion.97, bf16[1024,768]{1,0:T(8,128)(2,1)} %param.35, f32[768]{0:T(1024)} %copy-done.74, bf16[3,768,768]{2,1,0:T(8,128)(2,1)} %get-tuple-element.32, bf16[3,768,768]{2,1,0:T(8,128)(2,1)} %get-tuple-element.30), kind=kOutput, calls=%fused_computation.119 | convolution fusion | flops 2432434176 | bytes 10227712 | tf_op jit(solution)/shard_map/dot_general | solution.py:26
  282.1 11.5 %multiply_reduce_fusion.2 = (f32[768]{0:T(1024)}, f32[1024]{0:T(1024)S(1)}, f32[768]{0:T(1024)}, f32[1024,768]{1,0:T(8,128)}) fusion(f32[1024,768]{1,0:T(8,128)} %copy-done.7, f32[1024]{0:T(1024)S(1)} %copy-done.48, f32[1024]{0:T(1024)S(1)} %copy-done.44, f32[768]{0:T(1024)S(1)} %copy-done.59, bf16[3,768,768]{2,1,0:T(8,128)(2,1)} %get-tuple-element.30, ...), kind=kOutput, calls=%fused_computation.93 | convolution fusion | flops 2441082368 | bytes 22831104 | tf_op jit(solution)/shard_map/dot_general | solution.py:26
  293.7 3.7 fusion.172
  297.5 0.8 convolution_convert_fusion
  298.3 4.8 fusion.44
  303.2 1.8 convert_reduce_fusion.3
  305.1 1.9 multiply_reduce_fusion
  307.1 1.4 multiply_convert_fusion
  308.4 1.1 convolution_multiply_fusion
  309.5 1.9 multiply_reduce_fusion.1
  311.5 1.5 multiply_convert_fusion.1
  313.0 1.1 convolution_multiply_fusion.1
  317.4 2.9 fusion.170
  320.4 2.9 fusion.186.refs_1_
  323.3 3.4 fusion.167.refs_2_
  326.6 1.3 fusion.187.refs_3_
  327.9 1.3 fusion.188.refs_4_
  329.2 1.3 fusion.189.refs_5_
  330.6 1.6 fusion.116.refs_6_
  333.2 0.8 pad.4.refs_7_
  334.0 166.1 %shard_map.309 = (f32[1024,768]{1,0:T(8,128)}, f32[768,768]{1,0:T(8,128)}, f32[768,768]{1,0:T(8,128)}, f32[192,768]{1,0:T(8,128)}, f32[192,768]{1,0:T(8,128)}, /...) custom-call(f32[1024,768]{1,0:T(8,128)} %get-tuple-element.81.refs_0_, f32[768,768]{1,0:T(8,128)} %fusion.186.refs_1_, ...), custom_call_target="tpu_custom_call" | custom-call | tf_op jit(solution)/shard_map/pallas_call | solution.py:337
  500.1 2.8 fusion.42
  503.0 1.4 fusion.166
  505.3 2.7 add_add_fusion.2
  507.9 1.7 slice_reduce_fusion
  509.6 1.4 fusion.175
  511.0 0.8 copy.49
  511.8 0.8 copy.50
  512.6 0.8 copy.51
  513.5 0.8 copy.52
  514.3 1.4 copy.53
  515.7 1.4 copy.54
  (231 shorter events, 15.6 us)
Async XLA Ops:
  0.7 22.4 %copy-start = (bf16[768,768]{1,0:T(8,128)(2,1)S(1)}, bf16[768,768]{1,0:T(8,128)(2,1)}, u32[]{:S(2)}) copy-start(bf16[768,768]{1,0:T(8,128)(2,1)} %param.31) | copy-start | bytes 3538948
  0.7 4.5 copy-start.4
  0.7 4.5 copy-start.63
  0.7 4.5 copy-start.45
  0.7 5.1 copy-start.29
  0.7 5.1 copy-start.77
  5.2 2.1 copy-start.35
  5.9 2.1 copy-start.9
  5.9 2.1 copy-start.60
  6.6 11.3 %copy-start.15 = (bf16[1024,192]{0,1:T(8,128)(2,1)}, bf16[1024,192]{0,1:T(8,128)(2,1)S(1)}, u32[]{:S(2)}) copy-start(bf16[1024,192]{0,1:T(8,128)(2,1)S(1)} %fusion.80) | copy-start | bytes 1179652
  8.0 7.0 %copy-start.17 = (bf16[1024,192]{0,1:T(8,128)(2,1)}, bf16[1024,192]{0,1:T(8,128)(2,1)S(1)}, u32[]{:S(2)}) copy-start(bf16[1024,192]{0,1:T(8,128)(2,1)S(1)} %fusion.79) | copy-start | bytes 1179652
  10.6 2.7 copy-start.3
  10.6 2.7 copy-start.41
  16.4 2.6 copy-start.2
  16.4 2.6 copy-start.39
  19.0 1.7 copy-start.23
  20.7 8.2 %copy-start.66 = (f32[768]{0:T(1024)S(1)}, f32[768]{0:T(1024)}, u32[]{:S(2)}) copy-start(f32[768]{0:T(1024)} %param.32) | copy-start | bytes 9220
  23.1 178.8 %copy-start.64 = (f32[768]{0:T(1024)S(1)}, f32[768]{0:T(1024)}, u32[]{:S(2)}) copy-start(f32[768]{0:T(1024)} %param.28) | copy-start | bytes 9220
  204.8 6.0 %copy-start.51 = (f32[1024]{0:T(1024)}, f32[1024]{0:T(1024)S(1)}, u32[]{:S(2)}) copy-start(f32[1024]{0:T(1024)S(1)} %multiply_reduce_fusion.4) | copy-start | bytes 12292
  205.0 5.8 %copy-start.47 = (f32[1024]{0:T(1024)}, f32[1024]{0:T(1024)S(1)}, u32[]{:S(2)}) copy-start(f32[1024]{0:T(1024)S(1)} %fusion.131) | copy-start | bytes 12292
  205.9 4.9 copy-start.19
  215.3 6.1 %copy-start.20 = (bf16[1024,768]{1,0:T(8,128)(2,1)S(1)}, bf16[1024,768]{1,0:T(8,128)(2,1)}, u32[]{:S(2)}) copy-start(bf16[1024,768]{1,0:T(8,128)(2,1)} %copy-done.19) | copy-start | bytes 4718596
  222.8 3.8 copy-start.79
  226.6 4.4 copy-start.61
  233.1 6.0 %copy-start.74 = (f32[768]{0:T(1024)}, f32[768]{0:T(1024)S(1)}, u32[]{:S(2)}) copy-start(f32[768]{0:T(1024)S(1)} %add.261) | copy-start | bytes 9220
  233.1 6.0 %copy-start.21 = (bf16[1024,768]{1,0:T(8,128)(2,1)S(1)}, bf16[1024,768]{1,0:T(8,128)(2,1)}, u32[]{:S(2)}) copy-start(bf16[1024,768]{1,0:T(8,128)(2,1)} %copy-done.19) | copy-start | bytes 4718596
  244.3 9.6 %copy-start.75 = (f32[768]{0:T(1024)}, f32[768]{0:T(1024)S(1)}, u32[]{:S(2)}) copy-start(f32[768]{0:T(1024)S(1)} %add.274) | copy-start | bytes 9220
  244.3 9.6 %copy-start.42 = (f32[3,512]{1,0:T(4,128)S(1)}, f32[3,512]{1,0:T(4,128)}, u32[]{:S(2)}) copy-start(f32[3,512]{1,0:T(4,128)} %copy-done.41) | copy-start | bytes 18436
  244.3 9.6 %copy-start.56 = (f32[3,512]{1,0:T(4,128)S(1)}, f32[3,512]{1,0:T(4,128)}, u32[]{:S(2)}) copy-start(f32[3,512]{1,0:T(4,128)} %copy-done.55) | copy-start | bytes 18436
  253.9 8.6 %copy-start.68 = (f32[768]{0:T(1024)S(1)}, f32[768]{0:T(1024)}, u32[]{:S(2)}) copy-start(f32[768]{0:T(1024)} %param.32) | copy-start | bytes 9220
  273.1 9.0 %copy-start.44 = (f32[1024]{0:T(1024)S(1)}, f32[1024]{0:T(1024)}, u32[]{:S(2)}) copy-start(f32[1024]{0:T(1024)} %copy-done.43) | copy-start | bytes 12292
  273.1 9.0 %copy-start.48 = (f32[1024]{0:T(1024)S(1)}, f32[1024]{0:T(1024)}, u32[]{:S(2)}) copy-start(f32[1024]{0:T(1024)} %copy-done.47) | copy-start | bytes 12292
  273.1 9.0 %copy-start.59 = (f32[768]{0:T(1024)S(1)}, f32[768]{0:T(1024)}, u32[]{:S(2)}) copy-start(f32[768]{0:T(1024)} %param.29) | copy-start | bytes 9220
  273.1 9.0 %copy-start.76 = (f32[768]{0:T(1024)S(1)}, f32[768]{0:T(1024)}, u32[]{:S(2)}) copy-start(f32[768]{0:T(1024)} %copy-done.75) | copy-start | bytes 9220
  282.1 11.6 %copy-start.52 = (f32[1024]{0:T(1024)S(1)}, f32[1024]{0:T(1024)}, u32[]{:S(2)}) copy-start(f32[1024]{0:T(1024)} %copy-done.51) | copy-start | bytes 12292
  293.7 3.7 copy-start.11
  293.7 3.7 copy-start.24
  293.7 9.5 %slice-start = ((s8[6291456]{0:T(1024)(128)(4,1)}), s8[4194304]{0:T(1024)(128)(4,1)S(1)}, s32[]{:S(2)}) async-start(s8[6291456]{0:T(1024)(128)(4,1)} %bitcast.184), calls=%async_computation | async-start | bytes 8388608
  297.4 34.8 %copy-start.5 = (f32[1024,768]{1,0:T(8,128)}, f32[1024,768]{1,0:T(8,128)S(1)}, u32[]{:S(2)}) copy-start(f32[1024,768]{1,0:T(8,128)S(1)} %get-tuple-element.63) | copy-start | bytes 9437188
  297.5 34.7 %copy-start.37 = (f32[1024]{0:T(1024)}, f32[1024]{0:T(1024)S(1)}, u32[]{:S(2)}) copy-start(f32[1024]{0:T(1024)S(1)} %negate_multiply_fusion.1) | copy-start | bytes 12292
  297.5 5.7 %slice-start.1 = ((s8[6291456]{0:T(1024)(128)(4,1)}), s8[2097152]{0:T(1024)(128)(4,1)S(1)}, s32[]{:S(2)}) async-start(s8[6291456]{0:T(1024)(128)(4,1)} %bitcast.184), calls=%async_computation.1 | async-start | bytes 4194304
  298.3 4.9 copy-start.40
  298.3 4.9 copy-start.54
  298.3 6.8 %slice-start.2 = ((s8[6291456]{0:T(1024)(128)(4,1)}), s8[4194304]{0:T(1024)(128)(4,1)S(1)}, s32[]{:S(2)}) async-start(s8[6291456]{0:T(1024)(128)(4,1)} %bitcast.186), calls=%async_computation.2 | async-start | bytes 8388608
  303.2 1.9 slice-start.3
  303.2 1.9 copy-start.16
  317.4 3.0 copy-start.22
  317.4 2.9 copy-start.82
  320.4 2.9 copy-start.69
  320.4 2.9 copy-start.80
  323.3 3.4 copy-start.10
  334.0 166.1 %copy-start.46 = (f32[768]{0:T(1024)S(1)}, f32[768]{0:T(1024)}, u32[]{:S(2)}) copy-start(f32[768]{0:T(1024)} %param.20) | copy-start | bytes 9220
  500.1 2.8 copy-start.50
  500.1 2.9 copy-start.8
  502.9 1.9 copy-start.6
  502.9 2.3 copy-start.12
  503.0 2.3 copy-start.38
  505.3 5.7 %copy-start.28 = (f32[192,768]{1,0:T(8,128)S(1)}, f32[192,768]{1,0:T(8,128)}, u32[]{:S(2)}) copy-start(f32[192,768]{1,0:T(8,128)} %get-tuple-element.35) | copy-start | bytes 1769476
  505.3 6.6 %copy-start.27 = (f32[192,768]{1,0:T(8,128)S(1)}, f32[192,768]{1,0:T(8,128)}, u32[]{:S(2)}) copy-start(f32[192,768]{1,0:T(8,128)} %get-tuple-element.36) | copy-start | bytes 1769476
  505.3 7.4 %copy-start.26 = (f32[192,768]{1,0:T(8,128)S(1)}, f32[192,768]{1,0:T(8,128)}, u32[]{:S(2)}) copy-start(f32[192,768]{1,0:T(8,128)} %get-tuple-element.37) | copy-start | bytes 1769476
  507.9 5.5 %copy-start.25 = (f32[192,768]{1,0:T(8,128)S(1)}, f32[192,768]{1,0:T(8,128)}, u32[]{:S(2)}) copy-start(f32[192,768]{1,0:T(8,128)} %get-tuple-element.112) | copy-start | bytes 1769476
  507.9 6.3 %copy-start.14 = (f32[768,768]{1,0:T(8,128)S(1)}, f32[768,768]{1,0:T(8,128)}, u32[]{:S(2)}) copy-start(f32[768,768]{1,0:T(8,128)} %get-tuple-element.116) | copy-start | bytes 7077892
  513.5 2.2 copy-start.13
  514.3 2.8 copy-start.1
  (23 other events, 27.4 us)
